TPU v7x, 128 devices: a whole 4x4x4 slice. The times are simulated.
128 devices in a mesh: grp: 2 (over core), seq: 8 (over y_hi, z), dp: 8 (over x, y_lo).
Axes of the slice: x: 4, y: 4 (y_hi: 2, y_lo: 2; y = y_hi * 2 + y_lo), z: 4, core: 2. Of those that a mesh axis runs over, the one named last changes fastest.
Arguments:
- features: bfloat16 [8, 2, 8, 32, 16, 512], P('dp', None, None, ('grp', 'seq')), may hold values from -48 to 48
- group_gain: float32 [512], replicated, may hold values from 0.5 to 2
- group_bias: float32 [512], replicated, may hold values from -3 to 3
- conv_weight: bfloat16 [512, 432], replicated, may hold values from -0.0546875 to 0.0546875
- hidden: bfloat16 [2, 1, 8, 1024, 1920], P('grp', None, 'dp', 'seq'), may hold values from -36 to 36
- modulation: float32 [2, 1, 8, 3, 1920], P('grp', None, 'dp'), may hold values from -4 to 4
- timesteps: int32 [2, 1, 8], P('grp', None, 'dp'), may hold values from 0 to 999
- fresh_noise: float32 [2, 1, 8, 1024, 64], P('grp', None, 'dp', 'seq'), may hold values from -6 to 6
- input_weight: bfloat16 [1920, 3072], replicated, may hold values from -0.125 to 0.125
- query_gain: float32 [64], replicated, may hold values from 0.5 to 2
- key_gain: float32 [64], replicated, may hold values from 0.5 to 2
- output_weight: bfloat16 [1920, 1024], replicated, may hold values from -0.1875 to 0.1875
- patch_weight: bfloat16 [1920, 64], replicated, may hold values from -0.125 to 0.125
Outputs:
- weight_grad: float32 [1920, 3072], P(('grp', 'seq', 'dp'))
All inputs are finite; a program needn't handle non-finite values.
Results may differ from a plain program's by a relative error of at most 0.004.
Values may be sent and summed in bfloat16 or wider, within the bound.
A program may use at most 192 MiB of HBM per device.

v0:
```python
from functools import partial
import math

import jax
import jax.numpy as jnp
from jax import lax
from jax.sharding import PartitionSpec as P

HD = 64
HEADS = 16
GROUPS = 32
ZC = 16
TSTEPS = 1000


latent_scale = 1.15258426
group_eps = 1e-06
layer_eps = 1e-05
head_eps = 1e-06


def with_halo(array, sides, width):
    for axis, dim in sides:
        peers, length = (lax.axis_size(axis), array.shape[dim])
        up = [(i, (i + 1) % peers) for i in range(peers - 1)]
        down = [(j, i) for i, j in up]
        last = lax.slice_in_dim(array, length - width, length, axis=dim)
        first = lax.slice_in_dim(array, 0, width, axis=dim)
        before = lax.ppermute(last, axis, up)
        after = lax.ppermute(first, axis, down)
        array = jnp.concatenate([before, array, after], axis=dim)
    return array


def layer_norm(values, epsilon):
    average = jnp.mean(values, axis=-1, keepdims=True)
    centred = values - average
    variance = jnp.mean(centred * centred, axis=-1, keepdims=True)
    return centred * lax.rsqrt(variance + epsilon)


def head_norm(projected, head_gain):
    shaped = projected.reshape(projected.shape[:-1] + (HEADS, HD))
    return (layer_norm(shaped, head_eps) * head_gain).reshape(projected.shape)


def causal_conv(activated, conv_weight):
    frame_count = activated.shape[0]
    row_count = activated.shape[1] - 2
    col_count = activated.shape[2]
    padded = jnp.concatenate([activated[:1], activated[:1], activated], axis=0)
    padded = jnp.pad(padded, ((0, 0), (0, 0), (1, 1), (0, 0)))
    tap_terms = jnp.dot(
        padded.reshape(-1, padded.shape[-1]), conv_weight, preferred_element_type=jnp.float32
    )
    tap_terms = tap_terms.reshape(padded.shape[:3] + (27, ZC))
    total_sum = jnp.zeros((frame_count, row_count, col_count, ZC), jnp.float32)
    for time_tap in range(3):
        for row_tap in range(3):
            for column_tap in range(3):
                total_sum = (
                    total_sum
                    + tap_terms[
                        time_tap : time_tap + frame_count,
                        row_tap : row_tap + row_count,
                        column_tap : column_tap + col_count,
                        (time_tap * 3 + row_tap) * 3 + column_tap,
                    ]
                )
    return total_sum * latent_scale


def block_span(piece_rows, shard_rows):
    block_rows = shard_rows
    while block_rows < 512 and piece_rows % (block_rows * 2) == 0:
        block_rows = block_rows * 2
    return block_rows


def local(
    features,
    group_gain,
    group_bias,
    conv_weight,
    hidden,
    modulation,
    timesteps,
    fresh_noise,
    input_weight,
    query_gain,
    key_gain,
    output_weight,
    patch_weight,
):
    tile_block = features[0]
    clips_here, frame_count, row_count, col_count, channels = tile_block.shape
    grouped = tile_block.astype(jnp.float32).reshape(
        clips_here, frame_count, row_count, col_count, GROUPS, channels // GROUPS
    )
    average = jnp.mean(grouped, axis=(1, 2, 3, 5), keepdims=True)
    centred = grouped - average
    variance = jnp.mean(centred * centred, axis=(1, 2, 3, 5), keepdims=True)
    normed = (centred * lax.rsqrt(variance + group_eps)).reshape(
        tile_block.shape
    ) * group_gain + group_bias
    activated = jax.nn.silu(normed).astype(jnp.bfloat16)
    rimmed = with_halo(activated, ((("grp", "seq"), 2),), 1)
    latent = jax.vmap(partial(causal_conv, conv_weight=conv_weight))(rimmed)
    half_rows = row_count // 2
    half_cols = col_count // 2
    row_width = half_cols * 4 * ZC
    patches = latent.reshape(clips_here, frame_count, half_rows, 2, half_cols, 2, ZC).transpose(
        0, 1, 2, 4, 3, 5, 6
    )
    group_size = lax.axis_size("grp")
    per_core = clips_here // group_size
    patches = patches.reshape(group_size, per_core, frame_count, half_rows, row_width).transpose(
        0, 2, 1, 3, 4
    )
    patches = patches.reshape(group_size * frame_count * per_core, half_rows, row_width)
    relaid = lax.all_to_all(patches, ("grp", "seq"), split_axis=0, concat_axis=1, tiled=True)
    latent_tokens = relaid.reshape(per_core, -1, 4 * ZC)
    tokens = hidden[0, :, 0]
    adjust = modulation[0, :, 0]
    step_ids = timesteps[0, :, 0]
    noise_rows = fresh_noise[0, :, 0]
    tok_rows = tokens.shape[1]
    model_width = tokens.shape[2]
    inner_width = HEADS * HD
    seq_size = lax.axis_size("seq")
    shift_rows = adjust[:, 0:1]
    scale_rows = adjust[:, 1:2]
    gate_rows = adjust[:, 2:3]
    normed_tokens = (
        layer_norm(tokens.astype(jnp.float32), layer_eps) * (1.0 + scale_rows) + shift_rows
    ).astype(jnp.bfloat16)
    flat_normed = normed_tokens.reshape(per_core * tok_rows, model_width)
    projected = jnp.dot(flat_normed, input_weight, preferred_element_type=jnp.float32).reshape(
        per_core, tok_rows, 3 * inner_width
    )
    query_pre = projected[..., :inner_width]
    key_pre = projected[..., inner_width : 2 * inner_width]
    queries = head_norm(query_pre, query_gain).astype(jnp.bfloat16)
    key_rows = head_norm(key_pre, key_gain).astype(jnp.bfloat16)
    values = projected[..., 2 * inner_width :].astype(jnp.bfloat16)
    query_heads = queries.reshape(per_core, tok_rows, HEADS, HD)
    all_keys, all_values = (
        lax.all_gather(key_rows, "seq", axis=1, tiled=True),
        lax.all_gather(values, "seq", axis=1, tiled=True),
    )
    forward_total_sum = jnp.zeros((per_core, HEADS, tok_rows), jnp.float32)
    numerator = jnp.zeros((per_core, tok_rows, HEADS, HD), jnp.float32)
    piece_rows = all_keys.shape[1]
    block_rows = block_span(piece_rows, tok_rows)
    for offset in range(0, piece_rows, block_rows):
        block_keys = all_keys[:, offset : offset + block_rows].reshape(
            per_core, block_rows, HEADS, HD
        )
        block_values = all_values[:, offset : offset + block_rows].reshape(
            per_core, block_rows, HEADS, HD
        )
        scores = (
            jnp.einsum(
                "cqhd,ckhd->chqk", query_heads, block_keys, preferred_element_type=jnp.float32
            )
            * 0.125
        )
        exp_scores = jnp.exp(scores)
        forward_total_sum = forward_total_sum + jnp.sum(exp_scores, axis=-1)
        numerator = numerator + jnp.einsum(
            "chqk,ckhd->cqhd",
            exp_scores.astype(jnp.bfloat16),
            block_values,
            preferred_element_type=jnp.float32,
        )
    total_sum, numerator = (forward_total_sum, numerator)
    attended = (numerator / jnp.transpose(total_sum, (0, 2, 1))[..., None]).astype(jnp.bfloat16)
    flat_attended = attended.reshape(per_core * tok_rows, inner_width)
    branch = lax.dot_general(
        flat_attended, output_weight, (((1,), (1,)), ((), ())), preferred_element_type=jnp.float32
    )
    mixed_rows = tokens.astype(jnp.float32) + gate_rows * branch.reshape(
        per_core, tok_rows, model_width
    )
    final_rows, final_back = jax.vjp(partial(layer_norm, epsilon=layer_eps), mixed_rows)
    patch_count = patch_weight.shape[1]
    predicted = jnp.dot(
        final_rows.astype(jnp.bfloat16).reshape(-1, model_width),
        patch_weight,
        preferred_element_type=jnp.float32,
    )
    noise_angle = (step_ids.astype(jnp.float32) / TSTEPS + 0.008) / 1.008 * (math.pi / 2)
    target = (
        jnp.cos(noise_angle)[:, None, None] * noise_rows
        - jnp.sin(noise_angle)[:, None, None] * latent_tokens
    )
    pred_grad = (
        2.0 / patch_count * (predicted.reshape(per_core, tok_rows, patch_count) - target)
    ).astype(jnp.bfloat16)
    final_grad = lax.dot_general(
        pred_grad.reshape(-1, patch_count),
        patch_weight,
        (((1,), (1,)), ((), ())),
        preferred_element_type=jnp.float32,
    )
    mixed_grad = final_back(final_grad.reshape(per_core, tok_rows, model_width))[0]
    branch_grad = (gate_rows * mixed_grad).astype(jnp.bfloat16)
    attended_grad = jnp.dot(
        branch_grad.reshape(-1, model_width), output_weight, preferred_element_type=jnp.float32
    ).astype(jnp.bfloat16)
    attended_grad = attended_grad.reshape(per_core, tok_rows, HEADS, HD)
    delta_rows = jnp.transpose(
        jnp.sum(attended_grad.astype(jnp.float32) * attended.astype(jnp.float32), axis=-1),
        (0, 2, 1),
    )
    query_grad = jnp.zeros((per_core, tok_rows, HEADS, HD), jnp.float32)
    kv_partial = jnp.zeros((per_core, tok_rows * seq_size, 2 * inner_width), jnp.float32)
    piece_rows = all_keys.shape[1]
    block_rows = block_span(piece_rows, tok_rows)
    for offset in range(0, piece_rows, block_rows):
        block_keys = all_keys[:, offset : offset + block_rows].reshape(
            per_core, block_rows, HEADS, HD
        )
        block_values = all_values[:, offset : offset + block_rows].reshape(
            per_core, block_rows, HEADS, HD
        )
        scores = (
            jnp.einsum(
                "cqhd,ckhd->chqk", query_heads, block_keys, preferred_element_type=jnp.float32
            )
            * 0.125
        )
        probability = jnp.exp(scores) / total_sum[..., None]
        value_grad = jnp.einsum(
            "chqk,cqhd->ckhd",
            probability.astype(jnp.bfloat16),
            attended_grad,
            preferred_element_type=jnp.float32,
        )
        prob_grad = jnp.einsum(
            "cqhd,ckhd->chqk", attended_grad, block_values, preferred_element_type=jnp.float32
        )
        score_grad = (probability * (prob_grad - delta_rows[..., None])).astype(jnp.bfloat16)
        query_grad = (
            query_grad
            + jnp.einsum(
                "chqk,ckhd->cqhd", score_grad, block_keys, preferred_element_type=jnp.float32
            )
            * 0.125
        )
        key_grad = (
            jnp.einsum(
                "chqk,cqhd->ckhd", score_grad, query_heads, preferred_element_type=jnp.float32
            )
            * 0.125
        )
        block_grad = jnp.concatenate(
            [
                key_grad.reshape(per_core, block_rows, inner_width),
                value_grad.reshape(per_core, block_rows, inner_width),
            ],
            axis=2,
        )
        kv_partial = lax.dynamic_update_slice_in_dim(kv_partial, block_grad, 0 + offset, 1)
    query_grad, kv_partial = (query_grad, kv_partial)
    kv_grad = lax.psum_scatter(
        kv_partial.astype(jnp.bfloat16), "seq", scatter_dimension=1, tiled=True
    ).astype(jnp.float32)
    query_pre_grad = jax.vjp(partial(head_norm, head_gain=query_gain), query_pre)[1](
        query_grad.reshape(per_core, tok_rows, inner_width)
    )[0]
    key_pre_grad = jax.vjp(partial(head_norm, head_gain=key_gain), key_pre)[1](
        kv_grad[..., :inner_width]
    )[0]
    input_grad = jnp.concatenate(
        [query_pre_grad, key_pre_grad, kv_grad[..., inner_width:]], axis=2
    ).astype(jnp.bfloat16)
    input_grad = input_grad.reshape(per_core * tok_rows, 3 * inner_width)
    return lax.psum_scatter(
        lax.dot_general(
            flat_normed, input_grad, (((0,), (0,)), ((), ())), preferred_element_type=jnp.float32
        ),
        ("grp", "seq", "dp"),
        scatter_dimension=0,
        tiled=True,
    )


def solution(mesh):
    in_specs = (
        P("dp", None, None, ("grp", "seq"), None, None),
        P(),
        P(),
        P(),
        P("grp", None, "dp", "seq", None),
        P("grp", None, "dp", None, None),
        P("grp", None, "dp"),
        P("grp", None, "dp", "seq", None),
        P(),
        P(),
        P(),
        P(),
        P(),
    )
    out_specs = P(("grp", "seq", "dp"), None)
    return jax.shard_map(local, mesh=mesh, in_specs=in_specs, out_specs=out_specs, check_vma=False)
```

profile of v0, /device:TPU:56, one launch (start us, length us, event | category | flops | bytes accessed | tf_op | source)
XLA Modules:
  0.0 969.0 jit_solution(13990812451599265451)
XLA Ops:
  9.9 6.5 convolution_bitcast_fusion
  28.5 3.8 collective-permute-start
  38.6 4.9 collective-permute-done.1
  44.4 9.3 fusion.21
  53.7 32.2 %fusion.122 = (f32[2,8,2,16,1,16]{4,3,5,2,1,0:T(8,128)}, f32[2,8,2,16,1,16]{4,3,5,2,1,0:T(8,128)}, f32[2,8,2,16,1,16]{4,3,5,2,1,0:T(8,128)}, f32[2,8,2,16,1,16]{...) fusion(f32[2,10,4,18,27,16]{4,3,5,2,1,0:T(8,128)} %fusion.21), kind=kLoop, calls=%fused_computation.181 | loop fusion | bytes 655360 | tf_op jit(solution)/shard_map/vmap()/slice | solution.py:63
  85.9 4.7 copy.100
  90.6 4.8 copy.101
  95.4 4.7 copy.102
  100.2 4.8 copy.103
  104.9 4.7 copy.104
  109.6 5.4 copy.105
  115.0 5.5 copy.106
  120.6 5.4 copy.107
  126.0 5.4 copy.108
  131.3 5.4 copy.109
  136.7 37.6 %slice_add_fusion = f32[2,8,2,16,1,16]{4,3,5,2,1,0:T(8,128)} fusion(f32[2,10,4,18,27,16]{4,3,5,2,1,0:T(8,128)} %fusion.21), kind=kLoop, calls=%fused_computation.2 | loop fusion | flops 131072 | bytes 589824 | tf_op jit(solution)/shard_map/vmap()/add | solution.py:62
  174.4 5.4 copy.99
  182.4 10.1 %all-to-all-start = ((f32[16,1,512]{2,1,0:T(1,128)}), f32[16,1,512]{2,1,0:T(1,128)S(1)}, u32[]{:S(2)}, u32[]{:S(2)}) async-start(f32[16,1,512]{2,1,0:T(1,128)} %reshape_transpose_reshape.4), calls=%async_computation | async-start | bytes 65536 | tf_op jit(solution)/shard_map/all_to_all | solution.py:121
  202.4 4.4 fusion.4
  234.0 4.0 multiply_convert_fusion.1
  259.8 4.6 maximum_maximum_fusion
  271.3 76.5 %reduce-scatter.4.cloned.1.call-done = bf16[1,128,2048]{2,1,0:T(8,128)(2,1)} async-done(((bf16[1,1024,2048]{2,1,0:T(8,128)(2,1)}), bf16[1,128,2048]{2,1,0:T(8,128)(2,1)}) %reduce-scatter.4.cloned.1.call-update) | async-done | bytes 524304 | tf_op jit(solution)/shard_map/reduce_scatter | solution.py:266
  354.2 12.1 %fusion.84 = f32[1920,3072]{1,0:T(8,128)} fusion(bf16[128,1024]{1,0:T(8,128)(2,1)S(1)} %get-tuple-element.29, bf16[128,1024]{1,0:T(8,128)(2,1)S(1)} %fusion.100, bf16[128,1024]{1,0:T(8,128)(2,1)} %copy.123, bf16[1,1,1,128,1920]{4,3,2,1,0:T(8,128)(2,1)S(1)} %copy-done.2, f32[1920]{0:T(1024)S(1)} %get-tuple-element.6, f32[1920]{0:T(1024)S(1)} %get-tuple-element.7, ...), kind=kOutput, calls=%fused_computation.106 | convolution fusion | flops 1513783296 | bytes 24887296 | tf_op jit(solution)/shard_map/dot_general | solution.py:280
  366.3 540.3 %fusion = f32[16,3072]{1,0:T(8,128)S(1)} fusion(f32[1920,3072]{1,0:T(8,128)} %fusion.84), kind=kCustom, calls=%all-reduce-scatter | all-reduce-scatter fusion | flops 6291457 | bytes 23789568
  906.6 5.2 collective-permute-start.2
  917.5 5.8 collective-permute-start.4
  923.2 3.8 collective-permute-start.5
  927.1 3.5 collective-permute-done.9
  930.5 4.4 collective-permute-start.6
  936.9 7.2 collective-permute-start.8
  944.1 6.3 collective-permute-done.7
  954.3 7.0 concatenate.45
  (198 shorter events, 108.3 us)
Async XLA Ops:
  6.5 37.8 %copy-start = (bf16[512,432]{0,1:T(8,128)(2,1)S(1)}, bf16[512,432]{0,1:T(8,128)(2,1)}, u32[]{:S(2)}) copy-start(bf16[512,432]{0,1:T(8,128)(2,1)} %param.16) | copy-start | bytes 1327108
  6.5 190.1 %all-gather.3.cloned.1.call-start = ((), (), s32[]{:S(2)}) async-start(), calls=%async_computation.2 | async-start | bytes 2359296 | tf_op jit(solution)/shard_map/all_gather | solution.py:148
  8.6 7.8 copy-start.27
  9.9 6.5 copy-start.29
  17.9 4.9 copy-start.31
  17.9 4.9 copy-start.35
  19.3 6.2 copy-start.11
  19.6 7.0 copy-start.33
  19.6 7.0 copy-start.34
  22.7 21.6 %copy-start.12 = (f32[1,128,1024]{2,1,0:T(8,128)}, f32[1,128,1024]{2,1,0:T(8,128)S(1)}, u32[]{:S(2)}) copy-start(f32[1,128,1024]{2,1,0:T(8,128)S(1)} %copy.86) | copy-start | bytes 1572868
  25.5 184.1 %all-gather.5.cloned.1.call-start = ((), (), s32[]{:S(2)}) async-start(), calls=%async_computation.3 | async-start | bytes 2359296 | tf_op jit(solution)/shard_map/all_gather | solution.py:149
  28.5 10.1 %collective-permute-start = (bf16[2,8,1,16,512]{4,3,2,1,0:T(8,128)(2,1)}, bf16[2,8,1,16,512]{4,3,2,1,0:T(8,128)(2,1)S(1)}, u32[]{:S(2)}, u32[]{:S(2)}) collective-permute-start(bf16[2,8,1,16,512]{4,3,2,1,0:T(8,128)(2,1)} %get-tuple-element.30), channel_id=1, source_target_pairs={{0,8},{8,16},{16,24},{24,32},{32,40},{40,48},{48,56},{56,64},{64,7... | collective-permute-start | bytes 786440 | tf_op jit(solution)/shard_map/ppermute | solution.py:29
  32.3 11.2 %collective-permute-start.1 = (bf16[2,8,1,16,512]{4,3,2,1,0:T(8,128)(2,1)S(1)}, bf16[2,8,1,16,512]{4,3,2,1,0:T(8,128)(2,1)}, u32[]{:S(2)}, u32[]{:S(2)}) collective-permute-start(bf16[2,8,1,16,512]{4,3,2,1,0:T(8,128)(2,1)S(1)} %get-tuple-element.31), channel_id=1, source_target_pairs={{8,0},{16,8},{24,16},{32,24},{40,32},{48,40},{56,48},{64,56},{72,6... | collective-permute-start | bytes 786440 | tf_op jit(solution)/shard_map/ppermute | solution.py:30
  182.4 14.0 %all-to-all-start = ((f32[16,1,512]{2,1,0:T(1,128)}), f32[16,1,512]{2,1,0:T(1,128)S(1)}, u32[]{:S(2)}, u32[]{:S(2)}) async-start(f32[16,1,512]{2,1,0:T(1,128)} %reshape_transpose_reshape.4), calls=%async_computation | async-start | bytes 65536 | tf_op jit(solution)/shard_map/all_to_all | solution.py:121
  192.4 155.3 %reduce-scatter.4.cloned.1.call-start = ((), (), s32[]{:S(2)}) async-start(), calls=%async_computation.4 | async-start | bytes 4718592 | tf_op jit(solution)/shard_map/reduce_scatter | solution.py:266
  202.4 7.2 copy-start.8
  228.8 4.1 copy-start.19
  238.0 7.8 copy-start.10
  265.0 5.0 copy-start.23
  267.9 82.9 %copy-start.32 = (f32[64]{0:T(128)S(1)}, f32[64]{0:T(128)}, u32[]{:S(2)}) copy-start(f32[64]{0:T(128)} %param.23) | copy-start | bytes 772
  270.4 82.2 %copy-start.13 = (f32[1,128,1024]{2,1,0:T(8,128)S(1)}, f32[1,128,1024]{2,1,0:T(8,128)}, u32[]{:S(2)}) copy-start(f32[1,128,1024]{2,1,0:T(8,128)} %copy-done.12) | copy-start | bytes 1572868
  270.4 82.2 %copy-start.25 = (f32[1024]{0:T(1024)S(1)}, f32[1024]{0:T(1024)}, u32[]{:S(2)}) copy-start(f32[1024]{0:T(1024)} %copy-done.24) | copy-start | bytes 12292
  366.3 595.7 %copy-start.1 = (bf16[512,432]{0,1:T(8,128)(2,1)S(1)}, bf16[512,432]{0,1:T(8,128)(2,1)}, u32[]{:S(2)}) copy-start(bf16[512,432]{0,1:T(8,128)(2,1)} %param.16) | copy-start | bytes 1327108
  906.6 28.4 %collective-permute-start.2 = (f32[16,3072]{1,0:T(8,128)S(1)}, f32[16,3072]{1,0:T(8,128)S(1)}, u32[]{:S(2)}, u32[]{:S(2)}) collective-permute-start(f32[16,3072]{1,0:T(8,128)S(1)} %fusion), channel_id=1, source_target_pairs={{0,1},{1,2},{2,3},{3,4},{4,5},{5,6},{6,7},{7,8},{8,9},{9,10},{10,1... | collective-permute-start | bytes 589832
  911.7 25.1 %collective-permute-start.3 = (f32[16,3072]{1,0:T(8,128)S(1)}, f32[16,3072]{1,0:T(8,128)S(1)}, u32[]{:S(2)}, u32[]{:S(2)}) collective-permute-start(f32[16,3072]{1,0:T(8,128)S(1)} %fusion), channel_id=1, source_target_pairs={{0,2},{1,3},{2,4},{3,5},{4,6},{5,7},{6,8},{7,9},{8,10},{9,11},{10,... | collective-permute-start | bytes 589832
  914.8 15.7 %collective-permute-start.9 = (f32[15,3072]{1,0:T(8,128)S(1)}, f32[15,3072]{1,0:T(8,128)S(1)}, u32[]{:S(2)}, u32[]{:S(2)}) collective-permute-start(f32[15,3072]{1,0:T(8,128)S(1)} %slice.220), channel_id=1, source_target_pairs={{0,8},{1,9},{2,10},{3,11},{4,12},{5,13},{6,14},{7,15},{8,16},{9,17... | collective-permute-start | bytes 552968
  917.5 26.6 %collective-permute-start.4 = (f32[16,3072]{1,0:T(8,128)S(1)}, f32[16,3072]{1,0:T(8,128)S(1)}, u32[]{:S(2)}, u32[]{:S(2)}) collective-permute-start(f32[16,3072]{1,0:T(8,128)S(1)} %fusion), channel_id=1, source_target_pairs={{0,3},{1,4},{2,5},{3,6},{4,7},{5,8},{6,9},{7,10},{8,11},{9,12},{10... | collective-permute-start | bytes 589832
  923.2 20.8 %collective-permute-start.5 = (f32[16,3072]{1,0:T(8,128)S(1)}, f32[16,3072]{1,0:T(8,128)S(1)}, u32[]{:S(2)}, u32[]{:S(2)}) collective-permute-start(f32[16,3072]{1,0:T(8,128)S(1)} %fusion), channel_id=1, source_target_pairs={{0,4},{1,5},{2,6},{3,7},{4,8},{5,9},{6,10},{7,11},{8,12},{9,13},{1... | collective-permute-start | bytes 589832
  930.5 13.6 %collective-permute-start.6 = (f32[16,3072]{1,0:T(8,128)S(1)}, f32[16,3072]{1,0:T(8,128)S(1)}, u32[]{:S(2)}, u32[]{:S(2)}) collective-permute-start(f32[16,3072]{1,0:T(8,128)S(1)} %fusion), channel_id=1, source_target_pairs={{0,5},{1,6},{2,7},{3,8},{4,9},{5,10},{6,11},{7,12},{8,13},{9,14},{... | collective-permute-start | bytes 589832
  934.9 15.4 %collective-permute-start.7 = (f32[16,3072]{1,0:T(8,128)S(1)}, f32[16,3072]{1,0:T(8,128)S(1)}, u32[]{:S(2)}, u32[]{:S(2)}) collective-permute-start(f32[16,3072]{1,0:T(8,128)S(1)} %fusion), channel_id=1, source_target_pairs={{0,6},{1,7},{2,8},{3,9},{4,10},{5,11},{6,12},{7,13},{8,14},{9,15},... | collective-permute-start | bytes 589832
  936.9 17.4 %collective-permute-start.8 = (f32[16,3072]{1,0:T(8,128)S(1)}, f32[16,3072]{1,0:T(8,128)}, u32[]{:S(2)}, u32[]{:S(2)}) collective-permute-start(f32[16,3072]{1,0:T(8,128)S(1)} %fusion), channel_id=1, source_target_pairs={{0,7},{1,8},{2,9},{3,10},{4,11},{5,12},{6,13},{7,14},{8,15},{9,16}... | collective-permute-start | bytes 589832
  944.1 6.3 copy-start.20
  (19 other events, 47.4 us)
Sparse Core Ops, SparseCore 0:
  25.6 53.6 all-gather.2
  81.7 51.8 all-gather.4
  264.5 83.1 reduce-scatter.3
where the time goes:
time: 981 us; the launch traced here: 969 us
  blocking collectives  540 us (55%)
  local copies, waits for them, and re-layouts  138 us (14%)
  waiting for transfers between devices  99.8 us (10%)
  matrix products  66.4 us (7%)
  other arithmetic  58.8 us (6%)
  starting transfers between devices  49.9 us (5%)
  between operations  15.3 us (2%)
    unnamed x1, blocking collectives  540 us
    slice x11, local copies, waits for them, and re-layouts, causal_conv(): tap_terms[time_tap:time_tap + frame_count, row_tap:row_tap + row_count, c...  83.1 us
    reduce_scatter x1, waiting for transfers between devices, local(): lax.psum_scatter(kv_partial.astype(jnp.bfloat16), 'seq', scatter_dimensio...  76.5 us
    add x1, other arithmetic, causal_conv(): total_sum + tap_terms[time_tap:time_tap + frame_count, row_tap:row_tap +...  37.6 us
    unnamed x8, starting transfers between devices  33.9 us
  transfers between devices with their start and end apart: 14, of which 7 were waited for; matrix products, arithmetic and copies ran while one was open for 17% of the time, Pallas kernels for 0%

commit v1 on v0

v1 whole, which is shorter than its diff:
```python
import math

import jax
import jax.numpy as jnp
from jax import lax
from jax.experimental import pallas as pl
from jax.experimental.pallas import tpu as pltpu
from jax.sharding import PartitionSpec as P

F32 = jnp.float32
BF16 = jnp.bfloat16
MESH = pl.DeviceIdType.MESH

NG, NS, ND = 2, 8, 8
D = 1920
INNER = 1024
S = 1024
TOK = 128
W3 = 384
C = 512
HALF = D // NG
PART = HALF // ND
OUT_ROWS = 15
KB = 256
LATENT_SCALE = 1.15258426
GROUP_EPS = 1e-06
LAYER_EPS = 1e-05
HEAD_EPS = 1e-06


def mm(a, b):
    return lax.dot_general(a, b, (((1,), (0,)), ((), ())), preferred_element_type=F32)


def mm_nt(a, b):
    return lax.dot_general(a, b, (((1,), (1,)), ((), ())), preferred_element_type=F32)


def norm_rows(x):
    mu = jnp.mean(x, axis=-1, keepdims=True)
    centred = x - mu
    var = jnp.mean(centred * centred, axis=-1, keepdims=True)
    r = lax.rsqrt(var + LAYER_EPS)
    return centred * r, r


def head_norm_t(x):
    x3 = x.reshape(2, 64, x.shape[1])
    mu = jnp.mean(x3, axis=1, keepdims=True)
    centred = x3 - mu
    var = jnp.mean(centred * centred, axis=1, keepdims=True)
    r = lax.rsqrt(var + HEAD_EPS)
    return (centred * r).reshape(x.shape), r[:, 0, :]


def head_norm_back_t(grad, xhat, r):
    g3 = grad.reshape(2, 64, grad.shape[1])
    x3 = xhat.reshape(2, 64, grad.shape[1])
    mean_g = jnp.mean(g3, axis=1, keepdims=True)
    mean_gx = jnp.mean(g3 * x3, axis=1, keepdims=True)
    return ((g3 - mean_g - x3 * mean_gx) * r[:, None, :]).reshape(grad.shape)


def gain_columns(gain_row):
    both = jnp.concatenate([gain_row, gain_row], axis=1)
    return jnp.broadcast_to(both, (128, 128)).T


def group_mean(v, count):
    lane = lax.broadcasted_iota(jnp.int32, v.shape, 1)
    for step in (1, 2, 4, 8):
        up = pltpu.roll(v, C - step, 1)
        down = pltpu.roll(v, step, 1)
        v = v + jnp.where((lane & step) == 0, up, down)
    return v * (1.0 / count)


def kernel(
    trig,
    ggain,
    gbias,
    mod,
    qgain,
    kgain,
    feat_hbm,
    cw_hbm,
    hid_hbm,
    noise_hbm,
    w_hbm,
    wo_hbm,
    wp_hbm,
    out_ref,
    feat,
    cw,
    hid,
    noise,
    wq,
    wo,
    wp,
    ng,
    nT,
    wqT,
    taps,
    vsend,
    vrecv,
    lat,
    ltok,
    qT,
    kT,
    vT,
    qrow,
    kmask,
    vmask,
    xq,
    xk,
    rq,
    rk,
    eT,
    num,
    attT,
    att_row,
    att_tok,
    big,
    fin,
    rstd,
    tokbf,
    ag_tok,
    ag_head,
    agT,
    dqT,
    dk,
    dv,
    ig,
    wg_send,
    wg_own,
    sib,
    dpr,
    acc,
    fsend,
    frecv,
    ld_sem,
    ag_ss,
    ag_rs,
    lt_ss,
    lt_rs,
    a1_ss,
    a1_rs,
    a2_ss,
    a2_rs,
    sb_ss,
    sb_rs,
    dp_ss,
    dp_rs,
    fn_ss,
    fn_rs,
):
    g = lax.axis_index("grp")
    s = lax.axis_index("seq")
    d = lax.axis_index("dp")
    tile = g * NS + s

    def remote(src, dst, ssem, rsem, dev):
        return pltpu.make_async_remote_copy(
            src_ref=src, dst_ref=dst, send_sem=ssem, recv_sem=rsem, device_id=dev, device_id_type=MESH
        )

    def cols(index, width=128):
        return pl.ds(pl.multiple_of(index * width, width), width)

    loads = [
        pltpu.make_async_copy(hid_hbm, hid, ld_sem.at[0]),
        pltpu.make_async_copy(feat_hbm, feat, ld_sem.at[1]),
        pltpu.make_async_copy(cw_hbm, cw, ld_sem.at[2]),
        pltpu.make_async_copy(w_hbm.at[:, cols(s)], wq.at[:, 0:128], ld_sem.at[3]),
        pltpu.make_async_copy(w_hbm.at[:, cols(s + 8)], wq.at[:, 128:256], ld_sem.at[4]),
        pltpu.make_async_copy(w_hbm.at[:, cols(s + 16)], wq.at[:, 256:384], ld_sem.at[5]),
        pltpu.make_async_copy(noise_hbm, noise, ld_sem.at[6]),
        pltpu.make_async_copy(wo_hbm, wo, ld_sem.at[7]),
        pltpu.make_async_copy(wp_hbm, wp, ld_sem.at[8]),
    ]
    for copy in loads:
        copy.start()

    barrier = pltpu.get_barrier_semaphore()

    def greet(dev):
        pl.semaphore_signal(barrier, inc=1, device_id=dev, device_id_type=MESH)

    @pl.loop(1, 16)
    def _(j):
        t = lax.rem(tile + j, 16)
        greet((t // NS, lax.rem(t, NS), d))

    @pl.loop(1, 8)
    def _(j):
        greet((g, s, lax.rem(d + j, ND)))

    @pl.loop(0, 8)
    def _(j):
        me = jnp.logical_and(s == d, j == d)

        @pl.when(jnp.logical_not(me))
        def _():
            greet((g, d, j))
            greet((g, j, s))

    loads[0].wait()
    shift_row = mod[0:1, :]
    scale_row = 1.0 + mod[1:2, :]

    @pl.loop(0, TOK // 16)
    def _(i):
        rows = pl.ds(pl.multiple_of(i * 16, 16), 16)
        y, _ = norm_rows(hid[rows, :].astype(F32))
        ng[s, rows, :] = (y * scale_row + shift_row).astype(BF16)

    selfs = jnp.where(s == d, 2, 0)
    pl.semaphore_wait(barrier, 15 + 7 + 16 - selfs)

    def gather(j):
        peer = lax.rem(s + j, NS)
        return remote(ng.at[s], ng.at[s], ag_ss.at[j], ag_rs.at[s], (g, peer, d))

    @pl.loop(1, 8)
    def _(j):
        gather(j).start()

    loads[1].wait()
    loads[2].wait()
    row_id = lax.broadcasted_iota(jnp.int32, (432, W3), 0)
    col_id = lax.broadcasted_iota(jnp.int32, (432, W3), 1)
    inner = col_id & 127
    src0 = (col_id >> 7) * 144 + (inner >> 4) * 48 + (inner & 15)
    used = inner < 48
    cw_val = cw[...]
    col_w = lax.broadcasted_iota(jnp.int32, (C, C), 0) & 15
    acts = []
    for clip in range(2):
        x = feat[clip * 256 : clip * 256 + 256, :].astype(F32)
        mean = group_mean(jnp.broadcast_to(jnp.sum(x, axis=0, keepdims=True), (8, C)), 4096.0)[0:1]
        centred = x - mean
        var = group_mean(
            jnp.broadcast_to(jnp.sum(centred * centred, axis=0, keepdims=True), (8, C)), 4096.0
        )[0:1]
        normed = centred * lax.rsqrt(var + GROUP_EPS) * ggain[...] + gbias[...]
        acts.append(normed / (1.0 + jnp.exp(-normed)))
    act = jnp.concatenate(acts, axis=0)
    for e in range(3):
        pick = jnp.where(jnp.logical_and(used, row_id == src0 + e * 16), 1.0, 0.0).astype(BF16)
        we = mm(cw_val, pick).astype(BF16)
        if e == 0:
            ae = jnp.where(col_w == 0, 0.0, pltpu.roll(act, 1, 0))
        elif e == 2:
            ae = jnp.where(col_w == 15, 0.0, pltpu.roll(act, C - 1, 0))
        else:
            ae = act
        term = mm(ae.astype(BF16), we)
        if e == 0:
            taps[...] = term
        else:
            taps[...] += term
    for clip in range(2):
        for frame in range(8):
            total = None
            for a in range(3):
                base = (clip * 8 + max(frame + a - 2, 0)) * 32
                piece = taps[base : base + 32, a * 128 : a * 128 + 128]
                total = piece if total is None else total + piece
            vsend[clip * 8 + frame] = total
    vrecv[tile] = vsend[tile]

    def latent_copy(j):
        t = lax.rem(tile + j, 16)
        return remote(
            vsend.at[t], vrecv.at[tile], lt_ss.at[j], lt_rs.at[tile], (t // NS, lax.rem(t, NS), d)
        )

    @pl.loop(1, 16)
    def _(j):
        latent_copy(j).start()

    loads[3].wait()
    loads[4].wait()
    loads[5].wait()

    @pl.loop(0, 15)
    def _(i):
        wqT[:, cols(i)] = wq[cols(i), :].T

    gq = gain_columns(qgain[...])
    gk = gain_columns(kgain[...])
    low = lax.broadcasted_iota(jnp.int32, (128, 128), 1) < 64

    @pl.loop(0, 8)
    def _(j):
        src = lax.rem(s + 8 - j, NS)

        @pl.when(j > 0)
        def _():
            remote(ng.at[src], ng.at[src], ag_ss.at[j], ag_rs.at[src], (g, src, d)).wait_recv()

        here = cols(src)
        nt = ng[src].T
        nT[:, here] = nt
        pT = mm(wqT[...], nt)
        xhat, r = head_norm_t(pT[0:128])
        xq[:, here] = xhat
        rq[:, here] = r
        val = xhat * gq
        qT[:, here] = val.astype(BF16)
        qrow[here, :] = val.T.astype(BF16)
        xhat, r = head_norm_t(pT[128:256])
        xk[:, here] = xhat
        rk[:, here] = r
        val = xhat * gk
        kT[:, here] = val.astype(BF16)
        row = val.T
        kmask[0, here, :] = jnp.where(low, row, 0.0).astype(BF16)
        kmask[1, here, :] = jnp.where(low, 0.0, row).astype(BF16)
        val = pT[256:384]
        vT[:, here] = val.astype(BF16)
        row = val.T
        vmask[0, here, :] = jnp.where(low, row, 0.0).astype(BF16)
        vmask[1, here, :] = jnp.where(low, 0.0, row).astype(BF16)

    num[...] = jnp.zeros_like(num)

    def forward(c, tots):
        rows = cols(c, KB)
        new = []
        for h in range(2):
            e = jnp.exp(mm(kmask[h, rows, :], qT[...]) * 0.125)
            eT[h, rows, :] = e
            new.append(tots[h] + jnp.sum(e, axis=0, keepdims=True))
            hr = slice(h * 64, h * 64 + 64)
            num[hr, :] += mm(vT[hr, rows], e.astype(BF16))
        return tuple(new)

    zero_row = jnp.zeros((1, S), F32)
    tots = lax.fori_loop(0, S // KB, forward, (zero_row, zero_row))
    for h in range(2):
        hr = slice(h * 64, h * 64 + 64)
        num[hr, :] = num[hr, :] / tots[h]

    @pl.loop(0, 8)
    def _(j):
        here = cols(j)
        val = num[:, here]
        attT[:, here] = val.astype(BF16)
        att_row[here, :] = val.T.astype(BF16)

    def att_copy(j):
        peer = lax.rem(s + j, NS)
        return remote(
            att_row.at[cols(peer), :], att_tok.at[:, cols(s)], a1_ss.at[j], a1_rs.at[s], (g, peer, d)
        )

    @pl.loop(1, 8)
    def _(j):
        att_copy(j).start()

    att_tok[:, cols(s)] = att_row[cols(s), :]

    @pl.loop(1, 16)
    def _(j):
        t = lax.rem(tile + j, 16)
        remote(
            vsend.at[t], vrecv.at[t], lt_ss.at[j], lt_rs.at[t], (t // NS, lax.rem(t, NS), d)
        ).wait_recv()

    x = vrecv[...].reshape(512, 128)
    pad = jnp.zeros((16, 128), F32)
    total = jnp.concatenate([pad, x[:-16]], axis=0) + pltpu.roll(x, 112, 1)
    total = total + jnp.concatenate([pltpu.roll(x, 96, 1)[16:], pad], axis=0)
    lane = lax.broadcasted_iota(jnp.int32, (512, 128), 1)
    lat[...] = jnp.where(lane < 16, total * LATENT_SCALE, 0.0)
    tokens = jnp.zeros((128, 128), F32)
    for jj in range(2):
        half = lat[pl.ds(jj, 256, stride=2), :].reshape(16, 2, 8, 128)
        for ii in range(2):
            piece = half[:, ii].reshape(128, 128)
            place = 16 * (2 * ii + jj)
            tokens = tokens + (pltpu.roll(piece, place, 1) if place else piece)
    ltok[...] = tokens

    for index in (6, 7, 8):
        loads[index].wait()

    @pl.loop(1, 8)
    def _(j):
        src = lax.rem(s + 8 - j, NS)
        remote(
            att_row.at[cols(src), :], att_tok.at[:, cols(src)], a1_ss.at[j], a1_rs.at[src], (g, src, d)
        ).wait_recv()

    big[...] = mm_nt(att_tok[...], wo[...])
    gate_row = mod[2:3, :]

    @pl.loop(0, TOK // 16)
    def _(i):
        rows = pl.ds(pl.multiple_of(i * 16, 16), 16)
        mixed = hid[rows, :].astype(F32) + gate_row * big[rows, :]
        y, r = norm_rows(mixed)
        fin[rows, :] = y
        rstd[rows, :] = jnp.broadcast_to(r, (16, 128))
        tokbf[rows, :] = y.astype(BF16)

    target = trig[0] * noise[...] - trig[1] * ltok[:, 0:64]
    pred_grad = ((2.0 / 64) * (mm(tokbf[...], wp[...]) - target)).astype(BF16)
    big[...] = mm_nt(pred_grad, wp[...])

    @pl.loop(0, TOK // 16)
    def _(i):
        rows = pl.ds(pl.multiple_of(i * 16, 16), 16)
        dy = big[rows, :]
        y = fin[rows, :]
        mean_dy = jnp.mean(dy, axis=-1, keepdims=True)
        mean_dyy = jnp.mean(dy * y, axis=-1, keepdims=True)
        dx = (dy - mean_dy - y * mean_dyy) * rstd[rows, 0:1]
        tokbf[rows, :] = (gate_row * dx).astype(BF16)

    ag_tok[...] = mm(tokbf[...], wo[...]).astype(BF16)

    def ag_copy(j):
        peer = lax.rem(s + j, NS)
        return remote(
            ag_tok.at[:, cols(peer)], ag_head.at[cols(s), :], a2_ss.at[j], a2_rs.at[s], (g, peer, d)
        )

    @pl.loop(1, 8)
    def _(j):
        ag_copy(j).start()

    ag_head[cols(s), :] = ag_tok[:, cols(s)]

    @pl.loop(1, 8)
    def _(j):
        src = lax.rem(s + 8 - j, NS)
        remote(
            ag_tok.at[:, cols(src)], ag_head.at[cols(src), :], a2_ss.at[j], a2_rs.at[src], (g, src, d)
        ).wait_recv()

    @pl.loop(0, 8)
    def _(j):
        here = cols(j)
        val = ag_head[here, :].astype(F32).T
        agT[:, here] = val.astype(BF16)
        num[:, here] = val * attT[:, here].astype(F32)

    deltas = [jnp.sum(num[h * 64 : h * 64 + 64, :], axis=0, keepdims=True) for h in range(2)]
    invs = [1.0 / tots[h] for h in range(2)]
    dqT[...] = jnp.zeros_like(dqT)
    low_k = lax.broadcasted_iota(jnp.int32, (KB, 128), 1) < 64

    @pl.loop(0, S // KB)
    def _(c):
        rows = cols(c, KB)
        dvs = []
        dks = []
        for h in range(2):
            p = eT[h, rows, :] * invs[h]
            dp = mm(vmask[h, rows, :], agT[...])
            ds = (p * (dp - deltas[h])).astype(BF16)
            dvs.append(mm(p.astype(BF16), ag_head[...]))
            dks.append(mm(ds, qrow[...]))
            hr = slice(h * 64, h * 64 + 64)
            dqT[hr, :] += mm(kT[hr, rows], ds)
        dv[rows, :] = jnp.where(low_k, dvs[0], dvs[1])
        dk[rows, :] = jnp.where(low_k, dks[0], dks[1]) * 0.125

    @pl.loop(0, 8)
    def _(j):
        here = cols(j)
        grad = head_norm_back_t(dqT[:, here] * 0.125 * gq, xq[:, here], rq[:, here])
        ig[here, 0:128] = grad.T.astype(BF16)
        grad = head_norm_back_t(dk[here, :].T * gk, xk[:, here], rk[:, here])
        ig[here, 128:256] = grad.T.astype(BF16)
        ig[here, 256:384] = dv[here, :].astype(BF16)

    def sib_copy(i):
        return remote(wg_send.at[i], sib.at[i], sb_ss.at[i], sb_rs.at[i], (1 - g, s, d))

    @pl.loop(0, 4)
    def _(i):
        rows = pl.ds(pl.multiple_of((1 - g) * HALF + i * 240, 16), 240)
        wg_send[i] = mm(nT[rows, :], ig[...])
        sib_copy(i).start()

    @pl.loop(0, 4)
    def _(i):
        rows = pl.ds(pl.multiple_of(g * HALF + i * 240, 16), 240)
        value = mm(nT[rows, :], ig[...])
        wg_own[2 * i] = value[0:PART]
        wg_own[2 * i + 1] = value[PART : 2 * PART]

    def dp_copy(c):
        return remote(wg_own.at[c], dpr.at[d], dp_ss.at[c], dp_rs.at[d], (g, s, c))

    @pl.loop(0, 4)
    def _(j):
        i = lax.rem(d // 2 + 1 + j, 4)
        sib_copy(i).wait_recv()
        for q in range(2):
            c = 2 * i + q
            wg_own[c] += sib[i, q * PART : q * PART + PART, :]

            @pl.when(c != d)
            def _():
                dp_copy(c).start()

    acc[PART:, :] = jnp.zeros((128 - PART, W3), F32)
    acc[0:PART, :] = wg_own[d]

    @pl.loop(1, 8)
    def _(j):
        src = lax.rem(d + 8 - j, ND)
        remote(wg_own.at[src], dpr.at[src], dp_ss.at[src], dp_rs.at[src], (g, s, src)).wait_recv()
        acc[0:PART, :] += dpr[src]

    for j in range(8):
        fsend[j] = acc[j * OUT_ROWS : j * OUT_ROWS + 16, :]

    def fin_copy(j):
        return remote(fsend.at[j], frecv.at[s], fn_ss.at[j], fn_rs.at[s], (g, d, j))

    @pl.loop(0, 8)
    def _(j):
        me = jnp.logical_and(s == d, j == d)

        @pl.when(me)
        def _():
            frecv[s] = fsend[j]

        @pl.when(jnp.logical_not(me))
        def _():
            fin_copy(j).start()

    @pl.loop(0, 8)
    def _(j):
        me = jnp.logical_and(s == d, j == d)

        @pl.when(jnp.logical_not(me))
        def _():
            remote(fsend.at[j], frecv.at[j], fn_ss.at[j], fn_rs.at[j], (g, j, s)).wait_recv()

    for j in range(8):
        for part in range(3):
            out_ref[:, part * INNER + j * 128 : part * INNER + j * 128 + 128] = frecv[
                j, 0:OUT_ROWS, part * 128 : part * 128 + 128
            ]

    @pl.loop(1, 8)
    def _(j):
        gather(j).wait_send()
        att_copy(j).wait_send()
        ag_copy(j).wait_send()

    @pl.loop(1, 16)
    def _(j):
        latent_copy(j).wait_send()

    @pl.loop(0, 4)
    def _(i):
        sib_copy(i).wait_send()

    @pl.loop(0, 8)
    def _(c):
        @pl.when(c != d)
        def _():
            dp_copy(c).wait_send()

        me = jnp.logical_and(s == d, c == d)

        @pl.when(jnp.logical_not(me))
        def _():
            fin_copy(c).wait_send()


def scratch_shapes():
    V = pltpu.VMEM
    dma = pltpu.SemaphoreType.DMA
    return [
        V((512, C), BF16),
        V((C, 432), BF16),
        V((TOK, D), BF16),
        V((TOK, 64), F32),
        V((D, W3), BF16),
        V((D, INNER), BF16),
        V((D, 64), BF16),
        V((NS, TOK, D), BF16),
        V((D, S), BF16),
        V((W3, D), BF16),
        V((512, W3), F32),
        V((16, 32, 128), F32),
        V((16, 32, 128), F32),
        V((512, 128), F32),
        V((TOK, 128), F32),
        V((128, S), BF16),
        V((128, S), BF16),
        V((128, S), BF16),
        V((S, 128), BF16),
        V((2, S, 128), BF16),
        V((2, S, 128), BF16),
        V((128, S), F32),
        V((128, S), F32),
        V((2, S), F32),
        V((2, S), F32),
        V((2, S, S), F32),
        V((128, S), F32),
        V((128, S), BF16),
        V((S, 128), BF16),
        V((TOK, INNER), BF16),
        V((TOK, D), F32),
        V((TOK, D), F32),
        V((TOK, 128), F32),
        V((TOK, D), BF16),
        V((TOK, INNER), BF16),
        V((S, 128), BF16),
        V((128, S), BF16),
        V((128, S), F32),
        V((S, 128), F32),
        V((S, 128), F32),
        V((S, W3), BF16),
        V((4, 240, W3), F32),
        V((8, PART, W3), F32),
        V((4, 240, W3), F32),
        V((8, PART, W3), F32),
        V((128, W3), F32),
        V((8, 16, W3), F32),
        V((8, 16, W3), F32),
        dma((9,)),
        dma((8,)),
        dma((8,)),
        dma((16,)),
        dma((16,)),
        dma((8,)),
        dma((8,)),
        dma((8,)),
        dma((8,)),
        dma((4,)),
        dma((4,)),
        dma((8,)),
        dma((8,)),
        dma((8,)),
        dma((8,)),
    ]


def local(
    features,
    group_gain,
    group_bias,
    conv_weight,
    hidden,
    modulation,
    timesteps,
    fresh_noise,
    input_weight,
    query_gain,
    key_gain,
    output_weight,
    patch_weight,
):
    angle = (timesteps.reshape(1).astype(F32) / 1000 + 0.008) / 1.008 * (math.pi / 2)
    trig = jnp.concatenate([jnp.cos(angle), jnp.sin(angle)])
    vmem = pl.BlockSpec(memory_space=pltpu.VMEM)
    hbm = pl.BlockSpec(memory_space=pl.ANY)
    return pl.pallas_call(
        kernel,
        out_shape=jax.ShapeDtypeStruct((OUT_ROWS, 3 * INNER), F32),
        in_specs=[pl.BlockSpec(memory_space=pltpu.SMEM)] + [vmem] * 5 + [hbm] * 7,
        out_specs=vmem,
        scratch_shapes=scratch_shapes(),
        compiler_params=pltpu.CompilerParams(
            collective_id=0, has_side_effects=True, vmem_limit_bytes=60 * 2**20
        ),
    )(
        trig,
        group_gain.reshape(1, C),
        group_bias.reshape(1, C),
        modulation.reshape(3, D),
        query_gain.reshape(1, 64),
        key_gain.reshape(1, 64),
        features.reshape(512, C),
        conv_weight,
        hidden.reshape(TOK, D),
        fresh_noise.reshape(TOK, 64),
        input_weight,
        output_weight,
        patch_weight,
    )


def solution(mesh):
    in_specs = (
        P("dp", None, None, ("grp", "seq"), None, None),
        P(),
        P(),
        P(),
        P("grp", None, "dp", "seq", None),
        P("grp", None, "dp", None, None),
        P("grp", None, "dp"),
        P("grp", None, "dp", "seq", None),
        P(),
        P(),
        P(),
        P(),
        P(),
    )
    out_specs = P(("grp", "seq", "dp"), None)
    return jax.shard_map(local, mesh=mesh, in_specs=in_specs, out_specs=out_specs, check_vma=False)
```

time: 981 us -> 144 us (0.15); the launches traced: 969 us -> 143 us
  blocking collectives: 540 us -> 0 us
  Pallas kernels: 0 us -> 133 us
  local copies, waits for them, and re-layouts: 138 us -> 8.41 us
  waiting for transfers between devices: 99.8 us -> 0 us
  matrix products: 66.4 us -> 0 us
  other arithmetic: 58.8 us -> 0.58 us
  starting transfers between devices: 49.9 us -> 0 us
  between operations: 15.3 us -> 0.82 us
    unnamed x1 -> x0, blocking collectives: 540 us -> none
    pallas_call x0 -> x1, Pallas kernels: none -> 133 us  [local(): pl.pallas_call(kernel, out_shape=jax.ShapeDtypeStruct((OUT_ROWS, 3 * INNE...]
    slice x23 -> x0, local copies, waits for them, and re-layouts: 100 us -> none  [the longest x11 83.1 us: causal_conv(): tap_terms[time_tap:time_tap + frame_count, row_tap:row_tap + row_count, c...]
    reduce_scatter x1 -> x0, waiting for transfers between devices: 76.5 us -> none  [local(): lax.psum_scatter(kv_partial.astype(jnp.bfloat16), 'seq', scatter_dimensio...]
    dot_general x18 -> x0, matrix products: 66.4 us -> none  [the longest x1 12.1 us: local(): lax.dot_general(flat_normed, input_grad, (((0,), (0,)), ((), ())), prefer...]
    add x2 -> x0, other arithmetic: 37.6 us -> none  [the longest x1 37.6 us: causal_conv(): total_sum + tap_terms[time_tap:time_tap + frame_count, row_tap:row_tap +...]
    unnamed x8 -> x0, starting transfers between devices: 33.9 us -> none
    unnamed x11 -> x0, waiting for transfers between devices: 13 us -> none
  transfers between devices with their start and end apart: 14 -> 0, of which waited for: 7 -> 0; matrix products, arithmetic and copies ran while one was open for 17% -> 0% of each run, Pallas kernels for 0% -> 0%
where the time goes in v1:
time: 144 us; the launch traced here: 143 us
  Pallas kernels  133 us (92%)
  local copies, waits for them, and re-layouts  8.41 us (6%)
    pallas_call x1, Pallas kernels, local(): pl.pallas_call(kernel, out_shape=jax.ShapeDtypeStruct((OUT_ROWS, 3 * INNE...  133 us
    unnamed x5, local copies, waits for them, and re-layouts  8.41 us

profile of v1, /device:TPU:56, one launch (start us, length us, event | category | flops | bytes accessed | tf_op | source)
XLA Modules:
  0.0 143.0 jit_solution(10135449542618353281)
XLA Ops:
  0.8 0.6 pad_maximum_fusion.trig
  1.4 1.3 copy.19
  2.7 1.5 %copy.14 = f32[1,1,1,128,64]{4,3,2,1,0:T(8,128)} copy(f32[1,1,1,128,64]{3,4,2,1,0:T(8,128)} %param.20) | data formatting | bytes 65536 | tf_op args[7]
  4.2 1.9 %copy.16.wp_hbm = bf16[1920,64]{1,0:T(8,128)(2,1)} copy(bf16[1920,64]{0,1:T(8,128)(2,1)} %param.25) | data formatting | bytes 491520 | tf_op args[12]
  6.2 2.0 %copy.15.cw_hbm = bf16[512,432]{1,0:T(8,128)(2,1)} copy(bf16[512,432]{0,1:T(8,128)(2,1)} %param.16) | data formatting | bytes 884736 | tf_op args[3]
  8.2 133.2 %shard_map.127 = f32[15,3072]{1,0:T(8,128)} custom-call(f32[2]{0:T(128)} %pad_maximum_fusion.trig, f32[1,512]{1,0:T(1,128)} %bitcast.16, f32[1,512]{1,0:T(1,128)} %bitcast.17, f32[3,1920]{1,0:T(4,128)} %bitcast.15, f32[1,64]{1,0:T(1,128)} %bitcast.18, f32[1,64]{1,0:T(1,128)} %bitcast.19, bf16[512,512]{1,0:T(8,128)(2,1)} %bitcast.12, ...), custom_call_target="tpu_custom_call" | custom-call | tf_op jit(solution)/shard_map/pallas_call | solution.py:668
  141.4 1.6 %copy.22 = f32[15,3072]{1,0:T(8,128)} copy(f32[15,3072]{1,0:T(8,128)} %shard_map.127) | data formatting | bytes 368640

commit v2 on v1

--- a/solution.py
+++ b/solution.py
@@ -76,7 +76,7 @@
 
 
 def kernel(
-    trig,
+    steps,
     ggain,
     gbias,
     mod,
@@ -131,9 +131,9 @@
     dk,
     dv,
     ig,
-    wg_send,
+    ig_sib,
+    nT_sib,
     wg_own,
-    sib,
     dpr,
     acc,
     fsend,
@@ -153,6 +153,7 @@
     dp_rs,
     fn_ss,
     fn_rs,
+    nt_sem,
 ):
     g = lax.axis_index("grp")
     s = lax.axis_index("seq")
@@ -205,8 +206,8 @@
             greet((g, j, s))
 
     loads[0].wait()
-    shift_row = mod[0:1, :]
-    scale_row = 1.0 + mod[1:2, :]
+    shift_row = mod[0]
+    scale_row = 1.0 + mod[1]
 
     @pl.loop(0, TOK // 16)
     def _(i):
@@ -217,18 +218,27 @@
     selfs = jnp.where(s == d, 2, 0)
     pl.semaphore_wait(barrier, 15 + 7 + 16 - selfs)
 
-    def gather(j):
-        peer = lax.rem(s + j, NS)
-        return remote(ng.at[s], ng.at[s], ag_ss.at[j], ag_rs.at[s], (g, peer, d))
-
-    @pl.loop(1, 8)
-    def _(j):
-        gather(j).start()
+    yh, z = s // 4, lax.rem(s, 4)
+    z_up = yh * 4 + lax.rem(z + 1, 4)
+    z_down = yh * 4 + lax.rem(z + 3, 4)
+    across = (1 - yh) * 4 + z
+
+    def pass_on(slot, half, sem, peer):
+        block = ng.at[slot, pl.ds(half * 64, 64), :]
+        return remote(block, block, ag_ss.at[sem], ag_rs.at[slot * 2 + half], (g, peer, d))
+
+    own_sends = [
+        pass_on(s, half, half * 3 + k, peer)
+        for half in range(2)
+        for k, peer in enumerate((z_up, z_down, across))
+    ]
+    for copy in own_sends:
+        copy.start()
 
     loads[1].wait()
     loads[2].wait()
-    row_id = lax.broadcasted_iota(jnp.int32, (432, W3), 0)
-    col_id = lax.broadcasted_iota(jnp.int32, (432, W3), 1)
+    row_id = lax.broadcasted_iota(jnp.int32, (W3, 432), 1)
+    col_id = lax.broadcasted_iota(jnp.int32, (W3, 432), 0)
     inner = col_id & 127
     src0 = (col_id >> 7) * 144 + (inner >> 4) * 48 + (inner & 15)
     used = inner < 48
@@ -247,14 +257,14 @@
     act = jnp.concatenate(acts, axis=0)
     for e in range(3):
         pick = jnp.where(jnp.logical_and(used, row_id == src0 + e * 16), 1.0, 0.0).astype(BF16)
-        we = mm(cw_val, pick).astype(BF16)
+        we = mm(pick, cw_val).astype(BF16)
         if e == 0:
             ae = jnp.where(col_w == 0, 0.0, pltpu.roll(act, 1, 0))
         elif e == 2:
             ae = jnp.where(col_w == 15, 0.0, pltpu.roll(act, C - 1, 0))
         else:
             ae = act
-        term = mm(ae.astype(BF16), we)
+        term = mm_nt(ae.astype(BF16), we)
         if e == 0:
             taps[...] = term
         else:
@@ -293,11 +303,38 @@
 
     @pl.loop(0, 8)
     def _(j):
-        src = lax.rem(s + 8 - j, NS)
+        other = jnp.logical_or(j == 3, j >= 5)
+        hop = jnp.where(
+            jnp.logical_or(j == 1, j == 5), 3, jnp.where(jnp.logical_or(j == 2, j == 6), 1, 0)
+        )
+        hop = jnp.where(jnp.logical_or(j == 4, j == 7), 2, hop)
+        src = jnp.where(other, 1 - yh, yh) * 4 + lax.rem(z + hop, 4)
 
         @pl.when(j > 0)
         def _():
-            remote(ng.at[src], ng.at[src], ag_ss.at[j], ag_rs.at[src], (g, src, d)).wait_recv()
+            for half in range(2):
+                pass_on(src, half, 0, z_up).wait_recv()
+
+                if half == 0:
+
+                    @pl.when(j == 1)
+                    def _():
+                        pass_on(src, 0, 6, z_up).start()
+
+                else:
+
+                    @pl.when(j == 2)
+                    def _():
+                        pass_on(src, 1, 7, z_down).start()
+
+                @pl.when(j == 3)
+                def _():
+                    pass_on(src, half, 8 + 2 * half, z_up).start()
+                    pass_on(src, half, 9 + 2 * half, z_down).start()
+
+                @pl.when(j == 4)
+                def _():
+                    pass_on(src, half, 12 + half, across).start()
 
         here = cols(src)
         nt = ng[src].T
@@ -323,6 +360,15 @@
         vmask[0, here, :] = jnp.where(low, row, 0.0).astype(BF16)
         vmask[1, here, :] = jnp.where(low, 0.0, row).astype(BF16)
 
+    norm_copy = remote(
+        nT.at[pl.ds(pl.multiple_of((1 - g) * HALF, 16), HALF), :],
+        nT_sib,
+        nt_sem.at[0],
+        nt_sem.at[1],
+        (1 - g, s, d),
+    )
+    norm_copy.start()
+
     num[...] = jnp.zeros_like(num)
 
     def forward(c, tots):
@@ -394,7 +440,7 @@
         ).wait_recv()
 
     big[...] = mm_nt(att_tok[...], wo[...])
-    gate_row = mod[2:3, :]
+    gate_row = mod[2]
 
     @pl.loop(0, TOK // 16)
     def _(i):
@@ -405,9 +451,11 @@
         rstd[rows, :] = jnp.broadcast_to(r, (16, 128))
         tokbf[rows, :] = y.astype(BF16)
 
-    target = trig[0] * noise[...] - trig[1] * ltok[:, 0:64]
-    pred_grad = ((2.0 / 64) * (mm(tokbf[...], wp[...]) - target)).astype(BF16)
-    big[...] = mm_nt(pred_grad, wp[...])
+    step = jnp.full((TOK, 64), steps[0], jnp.int32).astype(F32)
+    angle = (step / 1000 + 0.008) / 1.008 * (math.pi / 2)
+    target = jnp.cos(angle) * noise[...].T - jnp.sin(angle) * ltok[:, 0:64]
+    pred_grad = ((2.0 / 64) * (mm_nt(tokbf[...], wp[...]) - target)).astype(BF16)
+    big[...] = mm(pred_grad, wp[...])
 
     @pl.loop(0, TOK // 16)
     def _(i):
@@ -468,6 +516,12 @@
         dv[rows, :] = jnp.where(low_k, dvs[0], dvs[1])
         dk[rows, :] = jnp.where(low_k, dks[0], dks[1]) * 0.125
 
+    def ig_copy(j):
+        here = cols(j)
+        return remote(
+            ig.at[here, :], ig_sib.at[here, :], sb_ss.at[j], sb_rs.at[j], (1 - g, s, d)
+        )
+
     @pl.loop(0, 8)
     def _(j):
         here = cols(j)
@@ -476,33 +530,26 @@
         grad = head_norm_back_t(dk[here, :].T * gk, xk[:, here], rk[:, here])
         ig[here, 128:256] = grad.T.astype(BF16)
         ig[here, 256:384] = dv[here, :].astype(BF16)
-
-    def sib_copy(i):
-        return remote(wg_send.at[i], sib.at[i], sb_ss.at[i], sb_rs.at[i], (1 - g, s, d))
+        ig_copy(j).start()
+
+    def dp_copy(c):
+        return remote(wg_own.at[c], dpr.at[d], dp_ss.at[c], dp_rs.at[d], (g, s, c))
+
+    @pl.loop(0, 8)
+    def _(j):
+        ig_copy(j).wait_recv()
+
+    norm_copy.wait_recv()
 
     @pl.loop(0, 4)
-    def _(i):
-        rows = pl.ds(pl.multiple_of((1 - g) * HALF + i * 240, 16), 240)
-        wg_send[i] = mm(nT[rows, :], ig[...])
-        sib_copy(i).start()
-
-    @pl.loop(0, 4)
-    def _(i):
+    def _(j):
+        i = lax.rem(d // 2 + 1 + j, 4)
         rows = pl.ds(pl.multiple_of(g * HALF + i * 240, 16), 240)
         value = mm(nT[rows, :], ig[...])
-        wg_own[2 * i] = value[0:PART]
-        wg_own[2 * i + 1] = value[PART : 2 * PART]
-
-    def dp_copy(c):
-        return remote(wg_own.at[c], dpr.at[d], dp_ss.at[c], dp_rs.at[d], (g, s, c))
-
-    @pl.loop(0, 4)
-    def _(j):
-        i = lax.rem(d // 2 + 1 + j, 4)
-        sib_copy(i).wait_recv()
+        value = value + mm(nT_sib[pl.ds(pl.multiple_of(i * 240, 16), 240), :], ig_sib[...])
         for q in range(2):
             c = 2 * i + q
-            wg_own[c] += sib[i, q * PART : q * PART + PART, :]
+            wg_own[c] = value[q * PART : q * PART + PART]
 
             @pl.when(c != d)
             def _():
@@ -549,19 +596,27 @@
                 j, 0:OUT_ROWS, part * 128 : part * 128 + 128
             ]
 
+    for copy in own_sends:
+        copy.wait_send()
+
+    @pl.loop(6, 14)
+    def _(sem):
+        pass_on(0, 0, sem, z_up).wait_send()
+
     @pl.loop(1, 8)
     def _(j):
-        gather(j).wait_send()
         att_copy(j).wait_send()
         ag_copy(j).wait_send()
 
+    @pl.loop(0, 8)
+    def _(j):
+        ig_copy(j).wait_send()
+
     @pl.loop(1, 16)
     def _(j):
         latent_copy(j).wait_send()
 
-    @pl.loop(0, 4)
-    def _(i):
-        sib_copy(i).wait_send()
+    norm_copy.wait_send()
 
     @pl.loop(0, 8)
     def _(c):
@@ -581,12 +636,12 @@
     dma = pltpu.SemaphoreType.DMA
     return [
         V((512, C), BF16),
-        V((C, 432), BF16),
+        V((432, C), BF16),
         V((TOK, D), BF16),
-        V((TOK, 64), F32),
+        V((64, TOK), F32),
         V((D, W3), BF16),
         V((D, INNER), BF16),
-        V((D, 64), BF16),
+        V((64, D), BF16),
         V((NS, TOK, D), BF16),
         V((D, S), BF16),
         V((W3, D), BF16),
@@ -621,28 +676,29 @@
         V((S, 128), F32),
         V((S, 128), F32),
         V((S, W3), BF16),
-        V((4, 240, W3), F32),
+        V((S, W3), BF16),
+        V((HALF, S), BF16),
         V((8, PART, W3), F32),
-        V((4, 240, W3), F32),
         V((8, PART, W3), F32),
         V((128, W3), F32),
         V((8, 16, W3), F32),
         V((8, 16, W3), F32),
         dma((9,)),
-        dma((8,)),
-        dma((8,)),
+        dma((14,)),
         dma((16,)),
         dma((16,)),
-        dma((8,)),
-        dma((8,)),
-        dma((8,)),
-        dma((8,)),
-        dma((4,)),
-        dma((4,)),
-        dma((8,)),
-        dma((8,)),
-        dma((8,)),
-        dma((8,)),
+        dma((16,)),
+        dma((8,)),
+        dma((8,)),
+        dma((8,)),
+        dma((8,)),
+        dma((8,)),
+        dma((8,)),
+        dma((8,)),
+        dma((8,)),
+        dma((8,)),
+        dma((8,)),
+        dma((2,)),
     ]
 
 
@@ -661,8 +717,6 @@
     output_weight,
     patch_weight,
 ):
-    angle = (timesteps.reshape(1).astype(F32) / 1000 + 0.008) / 1.008 * (math.pi / 2)
-    trig = jnp.concatenate([jnp.cos(angle), jnp.sin(angle)])
     vmem = pl.BlockSpec(memory_space=pltpu.VMEM)
     hbm = pl.BlockSpec(memory_space=pl.ANY)
     return pl.pallas_call(
@@ -675,19 +729,19 @@
             collective_id=0, has_side_effects=True, vmem_limit_bytes=60 * 2**20
         ),
     )(
-        trig,
+        timesteps.reshape(1),
         group_gain.reshape(1, C),
         group_bias.reshape(1, C),
-        modulation.reshape(3, D),
+        modulation.reshape(3, 1, D),
         query_gain.reshape(1, 64),
         key_gain.reshape(1, 64),
         features.reshape(512, C),
-        conv_weight,
+        conv_weight.T,
         hidden.reshape(TOK, D),
-        fresh_noise.reshape(TOK, 64),
+        fresh_noise.reshape(TOK, 64).T,
         input_weight,
         output_weight,
-        patch_weight,
+        patch_weight.T,
     )
 
 

time: 144 us -> 106 us (0.74)
  Pallas kernels: 133 us -> 102 us
  local copies, waits for them, and re-layouts: 8.41 us -> 1.62 us
    pallas_call x1, Pallas kernels: 133 us -> 102 us  [local(): pl.pallas_call(kernel, out_shape=jax.ShapeDtypeStruct((OUT_ROWS, 3 * INNE...]
    unnamed x5 -> x1, local copies, waits for them, and re-layouts: 8.41 us -> 1.62 us
where the time goes in v2:
time: 106 us; the launch traced here: 105 us
  Pallas kernels  102 us (96%)
  local copies, waits for them, and re-layouts  1.62 us (2%)
    pallas_call x1, Pallas kernels, local(): pl.pallas_call(kernel, out_shape=jax.ShapeDtypeStruct((OUT_ROWS, 3 * INNE...  102 us

profile of v2, /device:TPU:56, one launch (start us, length us, event | category | flops | bytes accessed | tf_op | source)
XLA Modules:
  0.0 104.6 jit_solution(6709038231065911975)
XLA Ops:
  0.7 102.3 %shard_map.127 = f32[15,3072]{1,0:T(8,128)} custom-call(s32[1]{0:T(128)} %bitcast.13.steps, f32[1,512]{1,0:T(1,128)} %bitcast.20, f32[1,512]{1,0:T(1,128)} %bitcast.21, f32[3,1,1920]{2,1,0:T(1,128)} %bitcast.19, f32[1,64]{1,0:T(1,128)} %bitcast.22, f32[1,64]{1,0:T(1,128)} %bitcast.23, bf16[512,512]{1,0:T(8,128)(2,1)} %bitcast.14, bf16[432,512]{1,0:T(8,128)(2,1)} %bitcast.16, ...), custom_call_target="tpu_custom_call" | custom-call | tf_op jit(solution)/shard_map/pallas_call | solution.py:722
  103.0 1.6 %copy.16 = f32[15,3072]{1,0:T(8,128)} copy(f32[15,3072]{1,0:T(8,128)} %shard_map.127) | data formatting | bytes 368640

commit v3 on v2

--- a/solution.py
+++ b/solution.py
@@ -129,15 +129,22 @@
     agT,
     dqT,
     dk,
-    dv,
     ig,
     ig_sib,
+    igv,
+    igv_sib,
     nT_sib,
-    wg_own,
-    dpr,
-    acc,
-    fsend,
-    frecv,
+    invs,
+    wgv,
+    wgq,
+    dpv,
+    dpq,
+    accv,
+    accq,
+    fsv,
+    fsq,
+    frv,
+    frq,
     ld_sem,
     ag_ss,
     ag_rs,
@@ -149,10 +156,16 @@
     a2_rs,
     sb_ss,
     sb_rs,
-    dp_ss,
-    dp_rs,
-    fn_ss,
-    fn_rs,
+    sv_ss,
+    sv_rs,
+    dv_ss,
+    dv_rs,
+    dq_ss,
+    dq_rs,
+    fv_ss,
+    fv_rs,
+    fq_ss,
+    fq_rs,
     nt_sem,
 ):
     g = lax.axis_index("grp")
@@ -369,41 +382,35 @@
     )
     norm_copy.start()
 
-    num[...] = jnp.zeros_like(num)
-
-    def forward(c, tots):
-        rows = cols(c, KB)
-        new = []
+    def att_copy(peer):
+        return remote(
+            att_row.at[cols(peer), :],
+            att_tok.at[:, cols(s)],
+            a1_ss.at[peer],
+            a1_rs.at[s],
+            (g, peer, d),
+        )
+
+    @pl.loop(0, S // KB)
+    def _(j):
+        c = lax.rem(s // 2 + 1 + j, S // KB)
+        here = cols(c, KB)
         for h in range(2):
-            e = jnp.exp(mm(kmask[h, rows, :], qT[...]) * 0.125)
-            eT[h, rows, :] = e
-            new.append(tots[h] + jnp.sum(e, axis=0, keepdims=True))
             hr = slice(h * 64, h * 64 + 64)
-            num[hr, :] += mm(vT[hr, rows], e.astype(BF16))
-        return tuple(new)
-
-    zero_row = jnp.zeros((1, S), F32)
-    tots = lax.fori_loop(0, S // KB, forward, (zero_row, zero_row))
-    for h in range(2):
-        hr = slice(h * 64, h * 64 + 64)
-        num[hr, :] = num[hr, :] / tots[h]
-
-    @pl.loop(0, 8)
-    def _(j):
-        here = cols(j)
+            e = jnp.exp(mm(kmask[h], qT[:, here]) * 0.125)
+            eT[h, :, here] = e
+            inv = 1.0 / jnp.sum(e, axis=0, keepdims=True)
+            invs[h : h + 1, here] = inv
+            num[hr, here] = mm(vT[hr, :], e.astype(BF16)) * inv
         val = num[:, here]
         attT[:, here] = val.astype(BF16)
         att_row[here, :] = val.T.astype(BF16)
-
-    def att_copy(j):
-        peer = lax.rem(s + j, NS)
-        return remote(
-            att_row.at[cols(peer), :], att_tok.at[:, cols(s)], a1_ss.at[j], a1_rs.at[s], (g, peer, d)
-        )
-
-    @pl.loop(1, 8)
-    def _(j):
-        att_copy(j).start()
+        for q in range(2):
+            peer = 2 * c + q
+
+            @pl.when(peer != s)
+            def _():
+                att_copy(peer).start()
 
     att_tok[:, cols(s)] = att_row[cols(s), :]
 
@@ -436,7 +443,7 @@
     def _(j):
         src = lax.rem(s + 8 - j, NS)
         remote(
-            att_row.at[cols(src), :], att_tok.at[:, cols(src)], a1_ss.at[j], a1_rs.at[src], (g, src, d)
+            att_row.at[cols(src), :], att_tok.at[:, cols(src)], a1_ss.at[src], a1_rs.at[src], (g, src, d)
         ).wait_recv()
 
     big[...] = mm_nt(att_tok[...], wo[...])
@@ -495,26 +502,75 @@
         agT[:, here] = val.astype(BF16)
         num[:, here] = val * attT[:, here].astype(F32)
 
-    deltas = [jnp.sum(num[h * 64 : h * 64 + 64, :], axis=0, keepdims=True) for h in range(2)]
-    invs = [1.0 / tots[h] for h in range(2)]
-    dqT[...] = jnp.zeros_like(dqT)
+    def v_copy(c):
+        rows = cols(c, KB)
+        return remote(
+            igv.at[rows, :], igv_sib.at[rows, :], sv_ss.at[c], sv_rs.at[c], (1 - g, s, d)
+        )
+
     low_k = lax.broadcasted_iota(jnp.int32, (KB, 128), 1) < 64
 
     @pl.loop(0, S // KB)
     def _(c):
         rows = cols(c, KB)
         dvs = []
+        for h in range(2):
+            p = eT[h, rows, :] * invs[h : h + 1, :]
+            dvs.append(mm(p.astype(BF16), ag_head[...]))
+        igv[rows, :] = jnp.where(low_k, dvs[0], dvs[1]).astype(BF16)
+        v_copy(c).start()
+
+    deltas = [jnp.sum(num[h * 64 : h * 64 + 64, :], axis=0, keepdims=True) for h in range(2)]
+    dqT[...] = jnp.zeros_like(dqT)
+
+    def score_back(c):
+        rows = cols(c, KB)
         dks = []
         for h in range(2):
-            p = eT[h, rows, :] * invs[h]
+            p = eT[h, rows, :] * invs[h : h + 1, :]
             dp = mm(vmask[h, rows, :], agT[...])
             ds = (p * (dp - deltas[h])).astype(BF16)
-            dvs.append(mm(p.astype(BF16), ag_head[...]))
             dks.append(mm(ds, qrow[...]))
             hr = slice(h * 64, h * 64 + 64)
             dqT[hr, :] += mm(kT[hr, rows], ds)
-        dv[rows, :] = jnp.where(low_k, dvs[0], dvs[1])
         dk[rows, :] = jnp.where(low_k, dks[0], dks[1]) * 0.125
+
+    @pl.loop(0, 2)
+    def _(c):
+        score_back(c)
+
+    def grad_rows(i, mine, theirs):
+        rows = pl.ds(pl.multiple_of(g * HALF + i * 240, 16), 240)
+        value = mm(nT[rows, :], mine[...])
+        return value + mm(nT_sib[pl.ds(pl.multiple_of(i * 240, 16), 240), :], theirs[...])
+
+    def dpv_copy(c):
+        return remote(wgv.at[c], dpv.at[d], dv_ss.at[c], dv_rs.at[d], (g, s, c))
+
+    def dpq_copy(c):
+        return remote(wgq.at[c], dpq.at[d], dq_ss.at[c], dq_rs.at[d], (g, s, c))
+
+    norm_copy.wait_recv()
+
+    @pl.loop(0, S // KB)
+    def _(c):
+        v_copy(c).wait_recv()
+
+    @pl.loop(0, 4)
+    def _(j):
+        i = lax.rem(d // 2 + 1 + j, 4)
+        value = grad_rows(i, igv, igv_sib)
+        for q in range(2):
+            c = 2 * i + q
+            wgv[c] = value[q * PART : q * PART + PART]
+
+            @pl.when(c != d)
+            def _():
+                dpv_copy(c).start()
+
+    @pl.loop(2, 4)
+    def _(c):
+        score_back(c)
 
     def ig_copy(j):
         here = cols(j)
@@ -529,72 +585,68 @@
         ig[here, 0:128] = grad.T.astype(BF16)
         grad = head_norm_back_t(dk[here, :].T * gk, xk[:, here], rk[:, here])
         ig[here, 128:256] = grad.T.astype(BF16)
-        ig[here, 256:384] = dv[here, :].astype(BF16)
         ig_copy(j).start()
 
-    def dp_copy(c):
-        return remote(wg_own.at[c], dpr.at[d], dp_ss.at[c], dp_rs.at[d], (g, s, c))
-
     @pl.loop(0, 8)
     def _(j):
         ig_copy(j).wait_recv()
 
-    norm_copy.wait_recv()
-
     @pl.loop(0, 4)
     def _(j):
         i = lax.rem(d // 2 + 1 + j, 4)
-        rows = pl.ds(pl.multiple_of(g * HALF + i * 240, 16), 240)
-        value = mm(nT[rows, :], ig[...])
-        value = value + mm(nT_sib[pl.ds(pl.multiple_of(i * 240, 16), 240), :], ig_sib[...])
+        value = grad_rows(i, ig, ig_sib)
         for q in range(2):
             c = 2 * i + q
-            wg_own[c] = value[q * PART : q * PART + PART]
+            wgq[c] = value[q * PART : q * PART + PART]
 
             @pl.when(c != d)
             def _():
-                dp_copy(c).start()
-
-    acc[PART:, :] = jnp.zeros((128 - PART, W3), F32)
-    acc[0:PART, :] = wg_own[d]
-
-    @pl.loop(1, 8)
-    def _(j):
-        src = lax.rem(d + 8 - j, ND)
-        remote(wg_own.at[src], dpr.at[src], dp_ss.at[src], dp_rs.at[src], (g, s, src)).wait_recv()
-        acc[0:PART, :] += dpr[src]
-
-    for j in range(8):
-        fsend[j] = acc[j * OUT_ROWS : j * OUT_ROWS + 16, :]
-
-    def fin_copy(j):
-        return remote(fsend.at[j], frecv.at[s], fn_ss.at[j], fn_rs.at[s], (g, d, j))
+                dpq_copy(c).start()
+
+    def finish_columns(own, arrived, part_sem, total, out_send, out_recv, send_sem, recv_sem):
+        total[PART:, :] = jnp.zeros((128 - PART, total.shape[1]), F32)
+        total[0:PART, :] = own[d]
+
+        @pl.loop(1, 8)
+        def _(j):
+            src = lax.rem(d + 8 - j, ND)
+            remote(own.at[src], arrived.at[src], part_sem.at[src], part_sem.at[src], (g, s, src)).wait_recv()
+            total[0:PART, :] += arrived[src]
+
+        for j in range(8):
+            out_send[j] = total[j * OUT_ROWS : j * OUT_ROWS + 16, :]
+
+        @pl.loop(0, 8)
+        def _(j):
+            me = jnp.logical_and(s == d, j == d)
+
+            @pl.when(me)
+            def _():
+                out_recv[s] = out_send[j]
+
+            @pl.when(jnp.logical_not(me))
+            def _():
+                remote(
+                    out_send.at[j], out_recv.at[s], send_sem.at[j], recv_sem.at[s], (g, d, j)
+                ).start()
+
+    finish_columns(wgv, dpv, dv_rs, accv, fsv, frv, fv_ss, fv_rs)
+    finish_columns(wgq, dpq, dq_rs, accq, fsq, frq, fq_ss, fq_rs)
 
     @pl.loop(0, 8)
     def _(j):
         me = jnp.logical_and(s == d, j == d)
-
-        @pl.when(me)
-        def _():
-            frecv[s] = fsend[j]
 
         @pl.when(jnp.logical_not(me))
         def _():
-            fin_copy(j).start()
-
-    @pl.loop(0, 8)
-    def _(j):
-        me = jnp.logical_and(s == d, j == d)
-
-        @pl.when(jnp.logical_not(me))
-        def _():
-            remote(fsend.at[j], frecv.at[j], fn_ss.at[j], fn_rs.at[j], (g, j, s)).wait_recv()
+            remote(fsv.at[j], frv.at[j], fv_ss.at[j], fv_rs.at[j], (g, j, s)).wait_recv()
+            remote(fsq.at[j], frq.at[j], fq_ss.at[j], fq_rs.at[j], (g, j, s)).wait_recv()
 
     for j in range(8):
-        for part in range(3):
-            out_ref[:, part * INNER + j * 128 : part * INNER + j * 128 + 128] = frecv[
-                j, 0:OUT_ROWS, part * 128 : part * 128 + 128
-            ]
+        lanes = slice(j * 128, j * 128 + 128)
+        out_ref[:, lanes] = frq[j, 0:OUT_ROWS, 0:128]
+        out_ref[:, INNER + j * 128 : INNER + j * 128 + 128] = frq[j, 0:OUT_ROWS, 128:256]
+        out_ref[:, 2 * INNER + j * 128 : 2 * INNER + j * 128 + 128] = frv[j, 0:OUT_ROWS, :]
 
     for copy in own_sends:
         copy.wait_send()
@@ -605,12 +657,16 @@
 
     @pl.loop(1, 8)
     def _(j):
-        att_copy(j).wait_send()
+        att_copy(lax.rem(s + j, NS)).wait_send()
         ag_copy(j).wait_send()
 
     @pl.loop(0, 8)
     def _(j):
         ig_copy(j).wait_send()
+
+    @pl.loop(0, S // KB)
+    def _(c):
+        v_copy(c).wait_send()
 
     @pl.loop(1, 16)
     def _(j):
@@ -622,13 +678,15 @@
     def _(c):
         @pl.when(c != d)
         def _():
-            dp_copy(c).wait_send()
+            dpv_copy(c).wait_send()
+            dpq_copy(c).wait_send()
 
         me = jnp.logical_and(s == d, c == d)
 
         @pl.when(jnp.logical_not(me))
         def _():
-            fin_copy(c).wait_send()
+            remote(fsv.at[c], frv.at[s], fv_ss.at[c], fv_rs.at[s], (g, d, c)).wait_send()
+            remote(fsq.at[c], frq.at[s], fq_ss.at[c], fq_rs.at[s], (g, d, c)).wait_send()
 
 
 def scratch_shapes():
@@ -674,15 +732,22 @@
         V((128, S), BF16),
         V((128, S), F32),
         V((S, 128), F32),
-        V((S, 128), F32),
-        V((S, W3), BF16),
-        V((S, W3), BF16),
+        V((S, 256), BF16),
+        V((S, 256), BF16),
+        V((S, 128), BF16),
+        V((S, 128), BF16),
         V((HALF, S), BF16),
-        V((8, PART, W3), F32),
-        V((8, PART, W3), F32),
-        V((128, W3), F32),
-        V((8, 16, W3), F32),
-        V((8, 16, W3), F32),
+        V((2, S), F32),
+        V((8, PART, 128), F32),
+        V((8, PART, 256), F32),
+        V((8, PART, 128), F32),
+        V((8, PART, 256), F32),
+        V((128, 128), F32),
+        V((128, 256), F32),
+        V((8, 16, 128), F32),
+        V((8, 16, 256), F32),
+        V((8, 16, 128), F32),
+        V((8, 16, 256), F32),
         dma((9,)),
         dma((14,)),
         dma((16,)),
@@ -690,6 +755,12 @@
         dma((16,)),
         dma((8,)),
         dma((8,)),
+        dma((8,)),
+        dma((8,)),
+        dma((8,)),
+        dma((8,)),
+        dma((4,)),
+        dma((4,)),
         dma((8,)),
         dma((8,)),
         dma((8,)),

time: 106 us -> 97.5 us (0.920); the launches traced: 105 us -> 97.3 us
  Pallas kernels: 102 us -> 95 us
    pallas_call x1, Pallas kernels: 102 us -> 95 us  [local(): pl.pallas_call(kernel, out_shape=jax.ShapeDtypeStruct((OUT_ROWS, 3 * INNE...]
where the time goes in v3:
time: 97.5 us; the launch traced here: 97.3 us
  Pallas kernels  95 us (97%)
  local copies, waits for them, and re-layouts  1.62 us (2%)
    pallas_call x1, Pallas kernels, local(): pl.pallas_call(kernel, out_shape=jax.ShapeDtypeStruct((OUT_ROWS, 3 * INNE...  95 us

profile of v3, /device:TPU:56, one launch (start us, length us, event | category | flops | bytes accessed | tf_op | source)
XLA Modules:
  0.0 97.3 jit_solution(4233563634753228111)
XLA Ops:
  0.7 95.0 %shard_map.127 = f32[15,3072]{1,0:T(8,128)} custom-call(s32[1]{0:T(128)} %bitcast.13.steps, f32[1,512]{1,0:T(1,128)} %bitcast.20, f32[1,512]{1,0:T(1,128)} %bitcast.21, f32[3,1,1920]{2,1,0:T(1,128)} %bitcast.19, f32[1,64]{1,0:T(1,128)} %bitcast.22, f32[1,64]{1,0:T(1,128)} %bitcast.23, bf16[512,512]{1,0:T(8,128)(2,1)} %bitcast.14, bf16[432,512]{1,0:T(8,128)(2,1)} %bitcast.16, ...), custom_call_target="tpu_custom_call" | custom-call | tf_op jit(solution)/shard_map/pallas_call | solution.py:793
  95.7 1.6 %copy.16 = f32[15,3072]{1,0:T(8,128)} copy(f32[15,3072]{1,0:T(8,128)} %shard_map.127) | data formatting | bytes 368640

commit v4 on v3

--- a/solution.py
+++ b/solution.py
@@ -100,21 +100,18 @@
     ng,
     nT,
     wqT,
+    qkv_send,
+    qkvT,
+    r_send,
+    r_all,
     taps,
     vsend,
     vrecv,
     lat,
     ltok,
-    qT,
-    kT,
-    vT,
     qrow,
     kmask,
     vmask,
-    xq,
-    xk,
-    rq,
-    rk,
     eT,
     num,
     attT,
@@ -166,7 +163,13 @@
     fv_rs,
     fq_ss,
     fq_rs,
-    nt_sem,
+    nt_ss,
+    nt_rs,
+    w_sem,
+    q_ss,
+    q_rs,
+    r_ss,
+    r_rs,
 ):
     g = lax.axis_index("grp")
     s = lax.axis_index("seq")
@@ -181,18 +184,32 @@
     def cols(index, width=128):
         return pl.ds(pl.multiple_of(index * width, width), width)
 
+    yh, z = s // 4, lax.rem(s, 4)
+    over = (1 - yh) * 4
+    across = over + z
+    w_loads = [
+        pltpu.make_async_copy(
+            w_hbm.at[:, cols(owner + 8 * part)],
+            wq.at[:, who * W3 + part * 128 : who * W3 + part * 128 + 128],
+            w_sem.at[who * 3 + part],
+        )
+        for who, owner in enumerate((s, across))
+        for part in range(3)
+    ]
+    hid_load = pltpu.make_async_copy(hid_hbm, hid, ld_sem.at[0])
+    hid_load.start()
+    for copy in w_loads:
+        copy.start()
+
     loads = [
-        pltpu.make_async_copy(hid_hbm, hid, ld_sem.at[0]),
+        hid_load,
         pltpu.make_async_copy(feat_hbm, feat, ld_sem.at[1]),
         pltpu.make_async_copy(cw_hbm, cw, ld_sem.at[2]),
-        pltpu.make_async_copy(w_hbm.at[:, cols(s)], wq.at[:, 0:128], ld_sem.at[3]),
-        pltpu.make_async_copy(w_hbm.at[:, cols(s + 8)], wq.at[:, 128:256], ld_sem.at[4]),
-        pltpu.make_async_copy(w_hbm.at[:, cols(s + 16)], wq.at[:, 256:384], ld_sem.at[5]),
-        pltpu.make_async_copy(noise_hbm, noise, ld_sem.at[6]),
-        pltpu.make_async_copy(wo_hbm, wo, ld_sem.at[7]),
-        pltpu.make_async_copy(wp_hbm, wp, ld_sem.at[8]),
+        pltpu.make_async_copy(noise_hbm, noise, ld_sem.at[3]),
+        pltpu.make_async_copy(wo_hbm, wo, ld_sem.at[4]),
+        pltpu.make_async_copy(wp_hbm, wp, ld_sem.at[5]),
     ]
-    for copy in loads:
+    for copy in loads[1:]:
         copy.start()
 
     barrier = pltpu.get_barrier_semaphore()
@@ -222,7 +239,7 @@
     shift_row = mod[0]
     scale_row = 1.0 + mod[1]
 
-    @pl.loop(0, TOK // 16)
+    @pl.loop(0, TOK // 16, unroll=4)
     def _(i):
         rows = pl.ds(pl.multiple_of(i * 16, 16), 16)
         y, _ = norm_rows(hid[rows, :].astype(F32))
@@ -231,19 +248,27 @@
     selfs = jnp.where(s == d, 2, 0)
     pl.semaphore_wait(barrier, 15 + 7 + 16 - selfs)
 
-    yh, z = s // 4, lax.rem(s, 4)
     z_up = yh * 4 + lax.rem(z + 1, 4)
     z_down = yh * 4 + lax.rem(z + 3, 4)
-    across = (1 - yh) * 4 + z
 
     def pass_on(slot, half, sem, peer):
         block = ng.at[slot, pl.ds(half * 64, 64), :]
         return remote(block, block, ag_ss.at[sem], ag_rs.at[slot * 2 + half], (g, peer, d))
 
+    def arrived(slot, half):
+        pass_on(slot, half, 0, z_up).wait_recv()
+
+    z_two = yh * 4 + lax.rem(z + 2, 4)
+    over_up = over + lax.rem(z + 1, 4)
+    over_down = over + lax.rem(z + 3, 4)
+    over_two = over + lax.rem(z + 2, 4)
     own_sends = [
-        pass_on(s, half, half * 3 + k, peer)
-        for half in range(2)
-        for k, peer in enumerate((z_up, z_down, across))
+        pass_on(s, 0, 0, z_up),
+        pass_on(s, 1, 1, z_down),
+        pass_on(s, 0, 2, across),
+        pass_on(s, 1, 3, z_up),
+        pass_on(s, 0, 4, z_down),
+        pass_on(s, 1, 5, across),
     ]
     for copy in own_sends:
         copy.start()
@@ -298,13 +323,21 @@
             vsend.at[t], vrecv.at[tile], lt_ss.at[j], lt_rs.at[tile], (t // NS, lax.rem(t, NS), d)
         )
 
-    @pl.loop(1, 16)
-    def _(j):
-        latent_copy(j).start()
-
-    loads[3].wait()
-    loads[4].wait()
-    loads[5].wait()
+    def norm_copy(slot):
+        return remote(
+            nT.at[pl.ds(pl.multiple_of((1 - g) * HALF, 16), HALF), cols(slot)],
+            nT_sib.at[:, cols(slot)],
+            nt_ss.at[slot],
+            nt_rs.at[slot],
+            (1 - g, s, d),
+        )
+
+    def take(slot):
+        nT[:, cols(slot)] = ng[slot].T
+        norm_copy(slot).start()
+
+    for copy in w_loads:
+        copy.wait()
 
     @pl.loop(0, 15)
     def _(i):
@@ -313,74 +346,100 @@
     gq = gain_columns(qgain[...])
     gk = gain_columns(kgain[...])
     low = lax.broadcasted_iota(jnp.int32, (128, 128), 1) < 64
-
-    @pl.loop(0, 8)
-    def _(j):
-        other = jnp.logical_or(j == 3, j >= 5)
-        hop = jnp.where(
-            jnp.logical_or(j == 1, j == 5), 3, jnp.where(jnp.logical_or(j == 2, j == 6), 1, 0)
+    r_send[...] = jnp.zeros_like(r_send)
+
+    def hop(j):
+        step = jnp.where(j == 1, 3, jnp.where(j == 2, 1, jnp.where(j == 3, 2, 0)))
+        return lax.rem(z + step, 4)
+
+    def qkv_copy(j, src):
+        return remote(
+            qkv_send.at[j], qkvT.at[:, cols(src)], q_ss.at[j], q_rs.at[src], (g, across, d)
         )
-        hop = jnp.where(jnp.logical_or(j == 4, j == 7), 2, hop)
-        src = jnp.where(other, 1 - yh, yh) * 4 + lax.rem(z + hop, 4)
-
-        @pl.when(j > 0)
-        def _():
-            for half in range(2):
-                pass_on(src, half, 0, z_up).wait_recv()
-
-                if half == 0:
-
-                    @pl.when(j == 1)
-                    def _():
-                        pass_on(src, 0, 6, z_up).start()
-
-                else:
-
-                    @pl.when(j == 2)
-                    def _():
-                        pass_on(src, 1, 7, z_down).start()
-
-                @pl.when(j == 3)
-                def _():
-                    pass_on(src, half, 8 + 2 * half, z_up).start()
-                    pass_on(src, half, 9 + 2 * half, z_down).start()
-
-                @pl.when(j == 4)
-                def _():
-                    pass_on(src, half, 12 + half, across).start()
-
-        here = cols(src)
-        nt = ng[src].T
-        nT[:, here] = nt
-        pT = mm(wqT[...], nt)
-        xhat, r = head_norm_t(pT[0:128])
-        xq[:, here] = xhat
-        rq[:, here] = r
-        val = xhat * gq
-        qT[:, here] = val.astype(BF16)
-        qrow[here, :] = val.T.astype(BF16)
-        xhat, r = head_norm_t(pT[128:256])
-        xk[:, here] = xhat
-        rk[:, here] = r
-        val = xhat * gk
-        kT[:, here] = val.astype(BF16)
-        row = val.T
+
+    def r_copy(j, src):
+        return remote(r_send.at[j], r_all.at[src], r_ss.at[j], r_rs.at[src], (g, across, d))
+
+    def rows_of(here, query, key, value):
+        qrow[here, :] = query.T.astype(BF16)
+        row = key.T
         kmask[0, here, :] = jnp.where(low, row, 0.0).astype(BF16)
         kmask[1, here, :] = jnp.where(low, 0.0, row).astype(BF16)
-        val = pT[256:384]
-        vT[:, here] = val.astype(BF16)
-        row = val.T
+        row = value.T
         vmask[0, here, :] = jnp.where(low, row, 0.0).astype(BF16)
         vmask[1, here, :] = jnp.where(low, 0.0, row).astype(BF16)
 
-    norm_copy = remote(
-        nT.at[pl.ds(pl.multiple_of((1 - g) * HALF, 16), HALF), :],
-        nT_sib,
-        nt_sem.at[0],
-        nt_sem.at[1],
-        (1 - g, s, d),
-    )
-    norm_copy.start()
+    @pl.loop(0, 4)
+    def _(j):
+        src = yh * 4 + hop(j)
+
+        @pl.when(j == 1)
+        def _():
+            arrived(z_down, 0)
+            pass_on(z_down, 0, 6, z_up).start()
+            arrived(z_up, 1)
+            pass_on(z_up, 1, 7, z_down).start()
+            arrived(z_down, 1)
+
+        @pl.when(j == 2)
+        def _():
+            arrived(z_up, 0)
+            for half in range(2):
+                arrived(across, half)
+                pass_on(across, half, 8 + 2 * half, z_up).start()
+                pass_on(across, half, 9 + 2 * half, z_down).start()
+
+        @pl.when(j == 3)
+        def _():
+            arrived(z_two, 0)
+            arrived(z_two, 1)
+
+        here = cols(src)
+        take(src)
+        pT = mm(wqT[...], nT[:, here])
+        for who in (1, 0):
+            base = who * W3
+            query, rq = head_norm_t(pT[base : base + 128])
+            key, rk = head_norm_t(pT[base + 128 : base + 256])
+            query = query * gq
+            key = key * gk
+            value = pT[base + 256 : base + 384]
+            if who == 1:
+                qkv_send[j, 0:128, :] = query.astype(BF16)
+                qkv_send[j, 128:256, :] = key.astype(BF16)
+                qkv_send[j, 256:384, :] = value.astype(BF16)
+                r_send[j, 0:2, :] = rq
+                r_send[j, 2:4, :] = rk
+                qkv_copy(j, src).start()
+                r_copy(j, src).start()
+            else:
+                qkvT[0:128, here] = query.astype(BF16)
+                qkvT[128:256, here] = key.astype(BF16)
+                qkvT[256:384, here] = value.astype(BF16)
+                r_all[src, 0:2, :] = rq
+                r_all[src, 2:4, :] = rk
+                rows_of(here, query, key, value)
+
+    @pl.loop(1, 16)
+    def _(j):
+        latent_copy(j).start()
+
+    @pl.loop(0, 4)
+    def _(j):
+        src = over + hop(j)
+        qkv_copy(j, src).wait_recv()
+        r_copy(j, src).wait_recv()
+        here = cols(src)
+        rows_of(
+            here,
+            qkvT[0:128, here].astype(F32),
+            qkvT[128:256, here].astype(F32),
+            qkvT[256:384, here].astype(F32),
+        )
+
+    qT = qkvT.at[0:128]
+    kT = qkvT.at[128:256]
+    vT = qkvT.at[256:384]
 
     def att_copy(peer):
         return remote(
@@ -436,7 +495,13 @@
             tokens = tokens + (pltpu.roll(piece, place, 1) if place else piece)
     ltok[...] = tokens
 
-    for index in (6, 7, 8):
+    arrived(over_down, 0)
+    pass_on(over_down, 0, 12, z_up).start()
+    arrived(over_up, 1)
+    pass_on(over_up, 1, 13, z_down).start()
+    take(across)
+
+    for index in (3, 4, 5):
         loads[index].wait()
 
     @pl.loop(1, 8)
@@ -449,7 +514,7 @@
     big[...] = mm_nt(att_tok[...], wo[...])
     gate_row = mod[2]
 
-    @pl.loop(0, TOK // 16)
+    @pl.loop(0, TOK // 16, unroll=4)
     def _(i):
         rows = pl.ds(pl.multiple_of(i * 16, 16), 16)
         mixed = hid[rows, :].astype(F32) + gate_row * big[rows, :]
@@ -464,7 +529,7 @@
     pred_grad = ((2.0 / 64) * (mm_nt(tokbf[...], wp[...]) - target)).astype(BF16)
     big[...] = mm(pred_grad, wp[...])
 
-    @pl.loop(0, TOK // 16)
+    @pl.loop(0, TOK // 16, unroll=4)
     def _(i):
         rows = pl.ds(pl.multiple_of(i * 16, 16), 16)
         dy = big[rows, :]
@@ -487,7 +552,6 @@
         ag_copy(j).start()
 
     ag_head[cols(s), :] = ag_tok[:, cols(s)]
-
     @pl.loop(1, 8)
     def _(j):
         src = lax.rem(s + 8 - j, NS)
@@ -550,7 +614,18 @@
     def dpq_copy(c):
         return remote(wgq.at[c], dpq.at[d], dq_ss.at[c], dq_rs.at[d], (g, s, c))
 
-    norm_copy.wait_recv()
+    arrived(over_down, 1)
+    arrived(over_up, 0)
+    arrived(over_two, 0)
+    arrived(over_two, 1)
+
+    @pl.loop(0, 3)
+    def _(j):
+        take(jnp.where(j == 0, over_down, jnp.where(j == 1, over_up, over_two)))
+
+    @pl.loop(0, 8)
+    def _(j):
+        norm_copy(j).wait_recv()
 
     @pl.loop(0, S // KB)
     def _(c):
@@ -572,6 +647,9 @@
     def _(c):
         score_back(c)
 
+    inv_gq = 1.0 / gq
+    inv_gk = 1.0 / gk
+
     def ig_copy(j):
         here = cols(j)
         return remote(
@@ -581,9 +659,11 @@
     @pl.loop(0, 8)
     def _(j):
         here = cols(j)
-        grad = head_norm_back_t(dqT[:, here] * 0.125 * gq, xq[:, here], rq[:, here])
+        xhat = qT[:, here].astype(F32) * inv_gq
+        grad = head_norm_back_t(dqT[:, here] * 0.125 * gq, xhat, r_all[j, 0:2, :])
         ig[here, 0:128] = grad.T.astype(BF16)
-        grad = head_norm_back_t(dk[here, :].T * gk, xk[:, here], rk[:, here])
+        xhat = kT[:, here].astype(F32) * inv_gk
+        grad = head_norm_back_t(dk[here, :].T * gk, xhat, r_all[j, 2:4, :])
         ig[here, 128:256] = grad.T.astype(BF16)
         ig_copy(j).start()
 
@@ -663,6 +743,12 @@
     @pl.loop(0, 8)
     def _(j):
         ig_copy(j).wait_send()
+        norm_copy(j).wait_send()
+
+    @pl.loop(0, 4)
+    def _(j):
+        qkv_copy(j, 0).wait_send()
+        r_copy(j, 0).wait_send()
 
     @pl.loop(0, S // KB)
     def _(c):
@@ -672,7 +758,6 @@
     def _(j):
         latent_copy(j).wait_send()
 
-    norm_copy.wait_send()
 
     @pl.loop(0, 8)
     def _(c):
@@ -697,27 +782,24 @@
         V((432, C), BF16),
         V((TOK, D), BF16),
         V((64, TOK), F32),
-        V((D, W3), BF16),
+        V((D, 2 * W3), BF16),
         V((D, INNER), BF16),
         V((64, D), BF16),
         V((NS, TOK, D), BF16),
         V((D, S), BF16),
-        V((W3, D), BF16),
+        V((2 * W3, D), BF16),
+        V((4, W3, TOK), BF16),
+        V((W3, S), BF16),
+        V((4, 8, TOK), F32),
+        V((NS, 8, TOK), F32),
         V((512, W3), F32),
         V((16, 32, 128), F32),
         V((16, 32, 128), F32),
         V((512, 128), F32),
         V((TOK, 128), F32),
-        V((128, S), BF16),
-        V((128, S), BF16),
-        V((128, S), BF16),
         V((S, 128), BF16),
         V((2, S, 128), BF16),
         V((2, S, 128), BF16),
-        V((128, S), F32),
-        V((128, S), F32),
-        V((2, S), F32),
-        V((2, S), F32),
         V((2, S, S), F32),
         V((128, S), F32),
         V((128, S), BF16),
@@ -748,7 +830,7 @@
         V((8, 16, 256), F32),
         V((8, 16, 128), F32),
         V((8, 16, 256), F32),
-        dma((9,)),
+        dma((6,)),
         dma((14,)),
         dma((16,)),
         dma((16,)),
@@ -769,7 +851,13 @@
         dma((8,)),
         dma((8,)),
         dma((8,)),
-        dma((2,)),
+        dma((8,)),
+        dma((8,)),
+        dma((6,)),
+        dma((8,)),
+        dma((8,)),
+        dma((8,)),
+        dma((8,)),
     ]
 
 

time: 97.5 us -> 90.8 us (0.931)
  Pallas kernels: 95 us -> 88.4 us
    pallas_call x1, Pallas kernels: 95 us -> 88.4 us  [local(): pl.pallas_call(kernel, out_shape=jax.ShapeDtypeStruct((OUT_ROWS, 3 * INNE...]
where the time goes in v4:
time: 90.8 us; the launch traced here: 90.6 us
  Pallas kernels  88.4 us (97%)
  local copies, waits for them, and re-layouts  1.62 us (2%)
    pallas_call x1, Pallas kernels, local(): pl.pallas_call(kernel, out_shape=jax.ShapeDtypeStruct((OUT_ROWS, 3 * INNE...  88.4 us

profile of v4, /device:TPU:56, one launch (start us, length us, event | category | flops | bytes accessed | tf_op | source)
XLA Modules:
  0.0 90.6 jit_solution(11220807416997618066)
XLA Ops:
  0.7 88.4 %shard_map.127 = f32[15,3072]{1,0:T(8,128)} custom-call(s32[1]{0:T(128)} %bitcast.13.steps, f32[1,512]{1,0:T(1,128)} %bitcast.20, f32[1,512]{1,0:T(1,128)} %bitcast.21, f32[3,1,1920]{2,1,0:T(1,128)} %bitcast.19, f32[1,64]{1,0:T(1,128)} %bitcast.22, f32[1,64]{1,0:T(1,128)} %bitcast.23, bf16[512,512]{1,0:T(8,128)(2,1)} %bitcast.14, bf16[432,512]{1,0:T(8,128)(2,1)} %bitcast.16, ...), custom_call_target="tpu_custom_call" | custom-call | tf_op jit(solution)/shard_map/pallas_call | solution.py:881
  89.0 1.6 %copy.16 = f32[15,3072]{1,0:T(8,128)} copy(f32[15,3072]{1,0:T(8,128)} %shard_map.127) | data formatting | bytes 368640

commit v5 on v4

--- a/solution.py
+++ b/solution.py
@@ -416,6 +416,7 @@
                 qkvT[0:128, here] = query.astype(BF16)
                 qkvT[128:256, here] = key.astype(BF16)
                 qkvT[256:384, here] = value.astype(BF16)
+                r_all[src] = jnp.zeros((8, TOK), F32)
                 r_all[src, 0:2, :] = rq
                 r_all[src, 2:4, :] = rk
                 rows_of(here, query, key, value)
@@ -608,6 +609,10 @@
         value = mm(nT[rows, :], mine[...])
         return value + mm(nT_sib[pl.ds(pl.multiple_of(i * 240, 16), 240), :], theirs[...])
 
+    def padded(value, q):
+        blank = jnp.zeros((128 - PART, value.shape[1]), F32)
+        return jnp.concatenate([value[q * PART : q * PART + PART], blank], axis=0)
+
     def dpv_copy(c):
         return remote(wgv.at[c], dpv.at[d], dv_ss.at[c], dv_rs.at[d], (g, s, c))
 
@@ -637,10 +642,15 @@
         value = grad_rows(i, igv, igv_sib)
         for q in range(2):
             c = 2 * i + q
-            wgv[c] = value[q * PART : q * PART + PART]
+            part = padded(value, q)
+
+            @pl.when(c == d)
+            def _():
+                accv[...] = part
 
             @pl.when(c != d)
             def _():
+                wgv[c] = part[0:PART]
                 dpv_copy(c).start()
 
     @pl.loop(2, 4)
@@ -677,21 +687,23 @@
         value = grad_rows(i, ig, ig_sib)
         for q in range(2):
             c = 2 * i + q
-            wgq[c] = value[q * PART : q * PART + PART]
+            part = padded(value, q)
+
+            @pl.when(c == d)
+            def _():
+                accq[...] = part
 
             @pl.when(c != d)
             def _():
+                wgq[c] = part.astype(BF16)
                 dpq_copy(c).start()
 
     def finish_columns(own, arrived, part_sem, total, out_send, out_recv, send_sem, recv_sem):
-        total[PART:, :] = jnp.zeros((128 - PART, total.shape[1]), F32)
-        total[0:PART, :] = own[d]
-
         @pl.loop(1, 8)
         def _(j):
             src = lax.rem(d + 8 - j, ND)
             remote(own.at[src], arrived.at[src], part_sem.at[src], part_sem.at[src], (g, s, src)).wait_recv()
-            total[0:PART, :] += arrived[src]
+            total[0 : arrived.shape[1], :] += arrived[src].astype(F32)
 
         for j in range(8):
             out_send[j] = total[j * OUT_ROWS : j * OUT_ROWS + 16, :]
@@ -821,9 +833,9 @@
         V((HALF, S), BF16),
         V((2, S), F32),
         V((8, PART, 128), F32),
-        V((8, PART, 256), F32),
+        V((8, 128, 256), BF16),
         V((8, PART, 128), F32),
-        V((8, PART, 256), F32),
+        V((8, 128, 256), BF16),
         V((128, 128), F32),
         V((128, 256), F32),
         V((8, 16, 128), F32),

time: 90.8 us -> 86.4 us (0.952); the launches traced: 90.6 us -> 85 us
  Pallas kernels: 88.4 us -> 82.7 us
    pallas_call x1, Pallas kernels: 88.4 us -> 82.7 us  [local(): pl.pallas_call(kernel, out_shape=jax.ShapeDtypeStruct((OUT_ROWS, 3 * INNE...]
where the time goes in v5:
time: 86.4 us; the launch traced here: 85 us
  Pallas kernels  82.7 us (96%)
  local copies, waits for them, and re-layouts  1.62 us (2%)
    pallas_call x1, Pallas kernels, local(): pl.pallas_call(kernel, out_shape=jax.ShapeDtypeStruct((OUT_ROWS, 3 * INNE...  82.7 us

profile of v5, /device:TPU:56, one launch (start us, length us, event | category | flops | bytes accessed | tf_op | source)
XLA Modules:
  0.0 85.0 jit_solution(4492800264606605889)
XLA Ops:
  0.7 82.7 %shard_map.127 = f32[15,3072]{1,0:T(8,128)} custom-call(s32[1]{0:T(128)} %bitcast.13.steps, f32[1,512]{1,0:T(1,128)} %bitcast.20, f32[1,512]{1,0:T(1,128)} %bitcast.21, f32[3,1,1920]{2,1,0:T(1,128)} %bitcast.19, f32[1,64]{1,0:T(1,128)} %bitcast.22, f32[1,64]{1,0:T(1,128)} %bitcast.23, bf16[512,512]{1,0:T(8,128)(2,1)} %bitcast.14, bf16[432,512]{1,0:T(8,128)(2,1)} %bitcast.16, ...), custom_call_target="tpu_custom_call" | custom-call | tf_op jit(solution)/shard_map/pallas_call | solution.py:893
  83.4 1.6 %copy.16 = f32[15,3072]{1,0:T(8,128)} copy(f32[15,3072]{1,0:T(8,128)} %shard_map.127) | data formatting | bytes 368640

commit v6 on v5

--- a/solution.py
+++ b/solution.py
@@ -99,7 +99,6 @@
     wp,
     ng,
     nT,
-    wqT,
     qkv_send,
     qkvT,
     r_send,
@@ -239,7 +238,7 @@
     shift_row = mod[0]
     scale_row = 1.0 + mod[1]
 
-    @pl.loop(0, TOK // 16, unroll=4)
+    @pl.loop(0, TOK // 16, unroll=8)
     def _(i):
         rows = pl.ds(pl.multiple_of(i * 16, 16), 16)
         y, _ = norm_rows(hid[rows, :].astype(F32))
@@ -339,10 +338,6 @@
     for copy in w_loads:
         copy.wait()
 
-    @pl.loop(0, 15)
-    def _(i):
-        wqT[:, cols(i)] = wq[cols(i), :].T
-
     gq = gain_columns(qgain[...])
     gk = gain_columns(kgain[...])
     low = lax.broadcasted_iota(jnp.int32, (128, 128), 1) < 64
@@ -395,15 +390,13 @@
             arrived(z_two, 1)
 
         here = cols(src)
-        take(src)
-        pT = mm(wqT[...], nT[:, here])
         for who in (1, 0):
-            base = who * W3
-            query, rq = head_norm_t(pT[base : base + 128])
-            key, rk = head_norm_t(pT[base + 128 : base + 256])
+            wide = mm(ng[src], wq[:, who * W3 : who * W3 + W3])
+            query, rq = head_norm_t(wide[:, 0:128].T)
+            key, rk = head_norm_t(wide[:, 128:256].T)
             query = query * gq
             key = key * gk
-            value = pT[base + 256 : base + 384]
+            value = wide[:, 256:384].T
             if who == 1:
                 qkv_send[j, 0:128, :] = query.astype(BF16)
                 qkv_send[j, 128:256, :] = key.astype(BF16)
@@ -420,6 +413,7 @@
                 r_all[src, 0:2, :] = rq
                 r_all[src, 2:4, :] = rk
                 rows_of(here, query, key, value)
+        take(src)
 
     @pl.loop(1, 16)
     def _(j):
@@ -474,6 +468,11 @@
 
     att_tok[:, cols(s)] = att_row[cols(s), :]
 
+    arrived(over_down, 0)
+    pass_on(over_down, 0, 12, z_up).start()
+    arrived(over_up, 1)
+    pass_on(over_up, 1, 13, z_down).start()
+
     @pl.loop(1, 16)
     def _(j):
         t = lax.rem(tile + j, 16)
@@ -496,11 +495,12 @@
             tokens = tokens + (pltpu.roll(piece, place, 1) if place else piece)
     ltok[...] = tokens
 
-    arrived(over_down, 0)
-    pass_on(over_down, 0, 12, z_up).start()
-    arrived(over_up, 1)
-    pass_on(over_up, 1, 13, z_down).start()
-    take(across)
+    arrived(over_down, 1)
+    arrived(over_up, 0)
+
+    @pl.loop(0, 3)
+    def _(j):
+        take(jnp.where(j == 0, across, jnp.where(j == 1, over_down, over_up)))
 
     for index in (3, 4, 5):
         loads[index].wait()
@@ -515,7 +515,7 @@
     big[...] = mm_nt(att_tok[...], wo[...])
     gate_row = mod[2]
 
-    @pl.loop(0, TOK // 16, unroll=4)
+    @pl.loop(0, TOK // 16, unroll=8)
     def _(i):
         rows = pl.ds(pl.multiple_of(i * 16, 16), 16)
         mixed = hid[rows, :].astype(F32) + gate_row * big[rows, :]
@@ -530,7 +530,7 @@
     pred_grad = ((2.0 / 64) * (mm_nt(tokbf[...], wp[...]) - target)).astype(BF16)
     big[...] = mm(pred_grad, wp[...])
 
-    @pl.loop(0, TOK // 16, unroll=4)
+    @pl.loop(0, TOK // 16, unroll=8)
     def _(i):
         rows = pl.ds(pl.multiple_of(i * 16, 16), 16)
         dy = big[rows, :]
@@ -540,24 +540,28 @@
         dx = (dy - mean_dy - y * mean_dyy) * rstd[rows, 0:1]
         tokbf[rows, :] = (gate_row * dx).astype(BF16)
 
-    ag_tok[...] = mm(tokbf[...], wo[...]).astype(BF16)
-
-    def ag_copy(j):
-        peer = lax.rem(s + j, NS)
+    def ag_copy(peer):
         return remote(
-            ag_tok.at[:, cols(peer)], ag_head.at[cols(s), :], a2_ss.at[j], a2_rs.at[s], (g, peer, d)
+            ag_tok.at[:, cols(peer)], ag_head.at[cols(s), :], a2_ss.at[peer], a2_rs.at[s], (g, peer, d)
         )
 
-    @pl.loop(1, 8)
-    def _(j):
-        ag_copy(j).start()
+    @pl.loop(0, 4)
+    def _(j):
+        c = lax.rem(s // 2 + 1 + j, 4)
+        ag_tok[:, cols(c, 256)] = mm(tokbf[...], wo[:, cols(c, 256)]).astype(BF16)
+        for q in range(2):
+            peer = 2 * c + q
+
+            @pl.when(peer != s)
+            def _():
+                ag_copy(peer).start()
 
     ag_head[cols(s), :] = ag_tok[:, cols(s)]
     @pl.loop(1, 8)
     def _(j):
         src = lax.rem(s + 8 - j, NS)
         remote(
-            ag_tok.at[:, cols(src)], ag_head.at[cols(src), :], a2_ss.at[j], a2_rs.at[src], (g, src, d)
+            ag_tok.at[:, cols(src)], ag_head.at[cols(src), :], a2_ss.at[src], a2_rs.at[src], (g, src, d)
         ).wait_recv()
 
     @pl.loop(0, 8)
@@ -604,9 +608,14 @@
     def _(c):
         score_back(c)
 
-    def grad_rows(i, mine, theirs):
+    def grad_rows(j, i, mine, theirs, wait_theirs):
         rows = pl.ds(pl.multiple_of(g * HALF + i * 240, 16), 240)
         value = mm(nT[rows, :], mine[...])
+
+        @pl.when(j == 0)
+        def _():
+            wait_theirs()
+
         return value + mm(nT_sib[pl.ds(pl.multiple_of(i * 240, 16), 240), :], theirs[...])
 
     def padded(value, q):
@@ -619,27 +628,29 @@
     def dpq_copy(c):
         return remote(wgq.at[c], dpq.at[d], dq_ss.at[c], dq_rs.at[d], (g, s, c))
 
-    arrived(over_down, 1)
-    arrived(over_up, 0)
     arrived(over_two, 0)
     arrived(over_two, 1)
 
-    @pl.loop(0, 3)
-    def _(j):
-        take(jnp.where(j == 0, over_down, jnp.where(j == 1, over_up, over_two)))
-
-    @pl.loop(0, 8)
-    def _(j):
-        norm_copy(j).wait_recv()
-
-    @pl.loop(0, S // KB)
-    def _(c):
-        v_copy(c).wait_recv()
+    take(over_two)
+
+    def wait_v():
+        @pl.loop(0, 8)
+        def _(j):
+            norm_copy(j).wait_recv()
+
+        @pl.loop(0, S // KB)
+        def _(c):
+            v_copy(c).wait_recv()
+
+    def wait_ig():
+        @pl.loop(0, 8)
+        def _(j):
+            ig_copy(j).wait_recv()
 
     @pl.loop(0, 4)
     def _(j):
         i = lax.rem(d // 2 + 1 + j, 4)
-        value = grad_rows(i, igv, igv_sib)
+        value = grad_rows(j, i, igv, igv_sib, wait_v)
         for q in range(2):
             c = 2 * i + q
             part = padded(value, q)
@@ -677,14 +688,10 @@
         ig[here, 128:256] = grad.T.astype(BF16)
         ig_copy(j).start()
 
-    @pl.loop(0, 8)
-    def _(j):
-        ig_copy(j).wait_recv()
-
     @pl.loop(0, 4)
     def _(j):
         i = lax.rem(d // 2 + 1 + j, 4)
-        value = grad_rows(i, ig, ig_sib)
+        value = grad_rows(j, i, ig, ig_sib, wait_ig)
         for q in range(2):
             c = 2 * i + q
             part = padded(value, q)
@@ -750,7 +757,7 @@
     @pl.loop(1, 8)
     def _(j):
         att_copy(lax.rem(s + j, NS)).wait_send()
-        ag_copy(j).wait_send()
+        ag_copy(lax.rem(s + j, NS)).wait_send()
 
     @pl.loop(0, 8)
     def _(j):
@@ -799,7 +806,6 @@
         V((64, D), BF16),
         V((NS, TOK, D), BF16),
         V((D, S), BF16),
-        V((2 * W3, D), BF16),
         V((4, W3, TOK), BF16),
         V((W3, S), BF16),
         V((4, 8, TOK), F32),

time: 86.4 us -> 85.2 us (0.986); the launches traced: 85 us -> 84.9 us
  no operation moved by 1% of the time
where the time goes in v6:
time: 85.2 us; the launch traced here: 84.9 us
  Pallas kernels  82.7 us (97%)
  local copies, waits for them, and re-layouts  1.62 us (2%)
    pallas_call x1, Pallas kernels, local(): pl.pallas_call(kernel, out_shape=jax.ShapeDtypeStruct((OUT_ROWS, 3 * INNE...  82.7 us

profile of v6, /device:TPU:56, one launch (start us, length us, event | category | flops | bytes accessed | tf_op | source)
XLA Modules:
  0.0 84.9 jit_solution(18058154505247210180)
XLA Ops:
  0.7 82.7 %shard_map.127 = f32[15,3072]{1,0:T(8,128)} custom-call(s32[1]{0:T(128)} %bitcast.13.steps, f32[1,512]{1,0:T(1,128)} %bitcast.20, f32[1,512]{1,0:T(1,128)} %bitcast.21, f32[3,1,1920]{2,1,0:T(1,128)} %bitcast.19, f32[1,64]{1,0:T(1,128)} %bitcast.22, f32[1,64]{1,0:T(1,128)} %bitcast.23, bf16[512,512]{1,0:T(8,128)(2,1)} %bitcast.14, bf16[432,512]{1,0:T(8,128)(2,1)} %bitcast.16, ...), custom_call_target="tpu_custom_call" | custom-call | tf_op jit(solution)/shard_map/pallas_call | solution.py:899
  83.3 1.6 %copy.16 = f32[15,3072]{1,0:T(8,128)} copy(f32[15,3072]{1,0:T(8,128)} %shard_map.127) | data formatting | bytes 368640
